TPU v7x, 256 devices: a whole 4x4x8 slice. The times are simulated.
256 devices in a mesh: var: 32 (over z_lo, x, core), tok: 8 (over y, z_hi).
Axes of the slice: x: 4, y: 4, z: 8 (z_hi: 2, z_lo: 4; z = z_hi * 4 + z_lo), core: 2. Of those that a mesh axis runs over, the one named last changes fastest.
Arguments:
- patches: bfloat16 [64, 64, 4096], P('var', None, 'tok'), may hold values from -6 to 6
- embed_weight: bfloat16 [64, 64, 1024], P('var'), may hold values from -0.75 to 0.75
- var_embed: float32 [64, 1024], P('var'), may hold values from -3 to 3
- agg_keys: bfloat16 [16, 1024], replicated, may hold values from -1.796875 to 1.796875
- agg_value: bfloat16 [1024, 1024], replicated, may hold values from -0.1875 to 0.1875
- agg_out: bfloat16 [1024, 1024], replicated, may hold values from -0.1875 to 0.1875
- pos_embed: bfloat16 [4096, 1024], P(('tok', 'var')), may hold values from -3 to 3
- norm_first: float32 [1024], replicated, may hold values from 0.5 to 1.5
- norm_second: float32 [1024], replicated, may hold values from 0.5 to 1.5
- w_qkv: bfloat16 [3, 1024, 1024], P(None, None, 'tok'), may hold values from -0.25 to 0.25
- w_out: bfloat16 [1024, 1024], P('tok'), may hold values from -0.1875 to 0.1875
- w_up: bfloat16 [1024, 4096], P(None, 'tok'), may hold values from -0.1875 to 0.1875
- w_down: bfloat16 [4096, 1024], P('tok'), may hold values from -0.09375 to 0.09375
- cotangent: bfloat16 [4096, 1024], P(('tok', 'var')), may hold values from -6 to 6
Outputs:
- block_out: bfloat16 [4096, 1024], P(('tok', 'var'))
- grad_embed: float32 [64, 64, 1024], P('var', None, 'tok')
- grad_var_embed: float32 [64, 1024], P('var', 'tok')
All inputs are finite; a program needn't handle non-finite values.
Results may differ from a plain program's by a relative error of at most 0.04.
Values may be sent and summed in bfloat16 or wider, within the bound.
A program may use at most 128 MiB of HBM per device.

v0:
```python
import jax
import jax.numpy as jnp
from jax import lax
from jax.sharding import PartitionSpec as P

EPS = 1e-05


def layer_norm(values, gain):
    mean = jnp.mean(values, axis=-1, keepdims=True)
    centred = values - mean
    spread = jnp.mean(centred * centred, axis=-1, keepdims=True)
    return centred * lax.rsqrt(spread + EPS) * gain


def smooth_gelu(values):
    return jax.nn.gelu(values, approximate=True)


def pool_forward(embedded, agg_keys, agg_value, agg_out):
    heads, width = agg_keys.shape
    size = width // heads
    scale = size ** (-0.5)
    scores = (
        jnp.einsum("vnd,hd->nhv", embedded, agg_keys, preferred_element_type=jnp.float32) * scale
    )
    expo = jnp.exp(scores)
    probs = expo / jnp.sum(expo, axis=-1, keepdims=True)
    probs_b = probs.astype(jnp.bfloat16)
    pooled = jnp.einsum(
        "nhv,vnd->nhd", probs_b, embedded, preferred_element_type=jnp.float32
    ).astype(jnp.bfloat16)
    value_three = agg_value.reshape(width, heads, size)
    picked = jnp.einsum(
        "nhd,dhe->nhe", pooled, value_three, preferred_element_type=jnp.float32
    ).astype(jnp.bfloat16)
    mixed = jnp.dot(picked.reshape(-1, width), agg_out, preferred_element_type=jnp.float32)
    return (mixed, (probs, probs_b))


def pool_backward(embedded, agg_keys, agg_value, agg_out, saved, grad_mixed):
    probs, probs_b = saved
    heads, width = agg_keys.shape
    size = width // heads
    scale = size ** (-0.5)
    grad_picked = jnp.einsum(
        "nk,dk->nd", grad_mixed, agg_out, preferred_element_type=jnp.float32
    ).astype(jnp.bfloat16)
    grad_picked = grad_picked.reshape(-1, heads, size)
    value_three = agg_value.reshape(width, heads, size)
    grad_pooled = jnp.einsum(
        "nhe,dhe->nhd", grad_picked, value_three, preferred_element_type=jnp.float32
    ).astype(jnp.bfloat16)
    grad_pool = jnp.einsum(
        "nhd,vnd->nhv", grad_pooled, embedded, preferred_element_type=jnp.float32
    )
    inner = jnp.sum(probs * grad_pool, axis=-1, keepdims=True)
    grad_pool_scores = (probs * (grad_pool - inner) * scale).astype(jnp.bfloat16)
    first = jnp.einsum("nhv,nhd->vnd", probs_b, grad_pooled, preferred_element_type=jnp.float32)
    second = jnp.einsum(
        "nhv,hd->vnd", grad_pool_scores, agg_keys, preferred_element_type=jnp.float32
    )
    return (first + second).astype(jnp.bfloat16)


def score_block(query, key_block, value_block, grad_att, total, delta, scale):
    scores = (
        jnp.einsum("rhe,khe->hrk", query, key_block, preferred_element_type=jnp.float32) * scale
    )
    probs = jnp.exp(scores) / total[:, :, None]
    grad_probs = jnp.einsum(
        "rhe,khe->hrk", grad_att, value_block, preferred_element_type=jnp.float32
    )
    grad_scores = (probs * (grad_probs - delta.T[:, :, None]) * scale).astype(jnp.bfloat16)
    return (probs.astype(jnp.bfloat16), grad_scores)


def local(
    patches,
    embed_weight,
    var_embed,
    agg_keys,
    agg_value,
    agg_out,
    pos_embed,
    norm_first,
    norm_second,
    w_qkv,
    w_out,
    w_up,
    w_down,
    cotangent,
):
    var_count = lax.axis_size("var")
    var_local, pixels, span = patches.shape
    width = embed_weight.shape[2]
    rows = span // var_count
    heads = agg_keys.shape[0]
    size = width // heads
    scale = size ** (-0.5)
    local_width = w_out.shape[0]
    local_heads = local_width // size
    embedded = jnp.einsum("vpn,vpd->vnd", patches, embed_weight, preferred_element_type=jnp.float32)
    embedded = (embedded + var_embed[:, None, :]).astype(jnp.bfloat16)
    arrived = lax.all_to_all(
        embedded.reshape(var_local, var_count, rows, width),
        "var",
        split_axis=1,
        concat_axis=0,
        tiled=True,
    )
    token_vars = arrived.reshape(var_local * var_count, rows, width)
    mixed, saved = pool_forward(token_vars, agg_keys, agg_value, agg_out)
    x_first = mixed + pos_embed.astype(jnp.float32)
    normed_first = layer_norm(x_first, norm_first).astype(jnp.bfloat16)
    qkv = jnp.einsum(
        "nd,sdc->nsc",
        lax.all_gather(normed_first, "tok", axis=0, tiled=True),
        w_qkv,
        preferred_element_type=jnp.float32,
    ).astype(jnp.bfloat16)
    group = qkv.shape[0]
    query = qkv[:, 0].reshape(group, local_heads, size)
    keys_values = lax.all_gather(qkv[:, 1:], "var", axis=0, tiled=True)
    seq = keys_values.shape[0]
    block = 2048
    count = seq // block
    steps = jnp.arange(count, dtype=jnp.int32)

    def key_piece(index):
        piece = lax.dynamic_slice_in_dim(keys_values, index * block, block, 0)
        return (
            piece[:, 0].reshape(block, local_heads, size),
            piece[:, 1].reshape(block, local_heads, size),
        )

    def forward_step(carry, index):
        numer, total = carry
        key_block, value_block = key_piece(index)
        scores = (
            jnp.einsum("rhe,khe->hrk", query, key_block, preferred_element_type=jnp.float32) * scale
        )
        expo = jnp.exp(scores)
        total = total + jnp.sum(expo, axis=-1)
        numer = numer + jnp.einsum(
            "hrk,khe->rhe",
            expo.astype(jnp.bfloat16),
            value_block,
            preferred_element_type=jnp.float32,
        )
        return ((numer, total), None)

    start_numer = jnp.zeros((group, local_heads, size), jnp.float32)
    start_total = jnp.zeros((local_heads, group), jnp.float32)
    (numer, total), _ = lax.scan(forward_step, (start_numer, start_total), steps)
    att = numer / total.T[:, :, None]
    att_b = att.astype(jnp.bfloat16).reshape(group, local_width)
    x_second = x_first + lax.psum_scatter(
        jnp.dot(att_b, w_out, preferred_element_type=jnp.float32).astype(jnp.bfloat16),
        "tok",
        scatter_dimension=0,
        tiled=True,
    ).astype(jnp.float32)
    normed_second = layer_norm(x_second, norm_second).astype(jnp.bfloat16)
    hidden_pre = jnp.dot(
        lax.all_gather(normed_second, "tok", axis=0, tiled=True),
        w_up,
        preferred_element_type=jnp.float32,
    )
    hidden = smooth_gelu(hidden_pre).astype(jnp.bfloat16)
    out_sum = x_second + lax.psum_scatter(
        jnp.dot(hidden, w_down, preferred_element_type=jnp.float32).astype(jnp.bfloat16),
        "tok",
        scatter_dimension=0,
        tiled=True,
    ).astype(jnp.float32)
    block_out = out_sum.astype(jnp.bfloat16)
    grad_hidden = jnp.einsum(
        "nd,fd->nf",
        lax.all_gather(cotangent, "tok", axis=0, tiled=True),
        w_down,
        preferred_element_type=jnp.float32,
    )
    _, gelu_back = jax.vjp(smooth_gelu, hidden_pre)
    grad_pre = gelu_back(grad_hidden)[0].astype(jnp.bfloat16)
    part = grad_pre
    grad_normed_second = lax.psum_scatter(
        jnp.einsum("nf,df->nd", part, w_up, preferred_element_type=jnp.float32).astype(
            jnp.bfloat16
        ),
        "tok",
        scatter_dimension=0,
        tiled=True,
    ).astype(jnp.float32)
    _, second_back = jax.vjp(lambda inner: layer_norm(inner, norm_second), x_second)
    grad_second = cotangent.astype(jnp.float32) + second_back(grad_normed_second)[0]
    grad_att_flat = jnp.einsum(
        "nd,cd->nc",
        lax.all_gather(grad_second.astype(jnp.bfloat16), "tok", axis=0, tiled=True),
        w_out,
        preferred_element_type=jnp.float32,
    ).astype(jnp.bfloat16)
    grad_att = grad_att_flat.reshape(group, local_heads, size)
    delta = jnp.sum(grad_att.astype(jnp.float32) * att, axis=-1)

    def backward_step(grad_query, index):
        key_block, value_block = key_piece(index)
        probs_b, grad_scores = score_block(
            query, key_block, value_block, grad_att, total, delta, scale
        )
        grad_query = grad_query + jnp.einsum(
            "hrk,khe->rhe", grad_scores, key_block, preferred_element_type=jnp.float32
        )
        grad_key = jnp.einsum(
            "hrk,rhe->khe", grad_scores, query, preferred_element_type=jnp.float32
        )
        grad_value = jnp.einsum(
            "hrk,rhe->khe", probs_b, grad_att, preferred_element_type=jnp.float32
        )
        return (
            grad_query,
            jnp.stack(
                [grad_key.reshape(block, local_width), grad_value.reshape(block, local_width)],
                axis=1,
            ),
        )

    grad_query, key_terms = lax.scan(backward_step, start_numer, steps)
    own_kv = lax.psum_scatter(
        key_terms.reshape(seq, 2, local_width).astype(jnp.bfloat16),
        "var",
        scatter_dimension=0,
        tiled=True,
    ).astype(jnp.float32)
    grad_qkv = jnp.concatenate([grad_query.reshape(group, 1, local_width), own_kv], axis=1).astype(
        jnp.bfloat16
    )
    part = grad_qkv
    grad_normed_first = lax.psum_scatter(
        jnp.einsum("nsc,sdc->nd", part, w_qkv, preferred_element_type=jnp.float32).astype(
            jnp.bfloat16
        ),
        "tok",
        scatter_dimension=0,
        tiled=True,
    ).astype(jnp.float32)
    _, first_back = jax.vjp(lambda inner: layer_norm(inner, norm_first), x_first)
    grad_first = grad_second + first_back(grad_normed_first)[0]
    grad_tokens = pool_backward(
        token_vars, agg_keys, agg_value, agg_out, saved, grad_first.astype(jnp.bfloat16)
    )
    returned = lax.all_to_all(
        grad_tokens.reshape(var_local * var_count, 1, rows, width),
        "var",
        split_axis=0,
        concat_axis=1,
        tiled=True,
    )
    grad_embedded = returned.reshape(var_local, span, width)
    embed_term = jnp.einsum(
        "vpn,vnd->vpd", patches, grad_embedded, preferred_element_type=jnp.float32
    )
    var_term = jnp.sum(grad_embedded, axis=1, dtype=jnp.float32)
    grad_embed, grad_var_embed = (
        lax.psum_scatter(
            embed_term.astype(jnp.bfloat16), "tok", scatter_dimension=2, tiled=True
        ).astype(jnp.float32),
        lax.psum_scatter(
            var_term.astype(jnp.bfloat16), "tok", scatter_dimension=1, tiled=True
        ).astype(jnp.float32),
    )
    return (block_out, grad_embed, grad_var_embed)


def solution(mesh):
    in_specs = (
        P("var", None, "tok"),
        P("var", None, None),
        P("var", None),
        P(),
        P(),
        P(),
        P(("tok", "var"), None),
        P(),
        P(),
        P(None, None, "tok"),
        P("tok", None),
        P(None, "tok"),
        P("tok", None),
        P(("tok", "var"), None),
    )
    out_specs = (P(("tok", "var"), None), P("var", None, "tok"), P("var", "tok"))
    return jax.shard_map(local, mesh=mesh, in_specs=in_specs, out_specs=out_specs, check_vma=False)
```

profile of v0, /device:TPU:1, one launch (start us, length us, event | category | flops | bytes accessed | tf_op | source)
XLA Modules:
  0.0 1041.4 jit_solution(1015444850351498541)
XLA Ops:
  10.5 10.1 all-to-all-start
  20.7 4.0 copy.73
  25.9 42.9 %all-to-all-done = bf16[2,32,16,1024]{3,2,0,1:T(8,128)(2,1)} async-done(((bf16[2,32,16,1024]{3,2,0,1:T(8,128)(2,1)}), bf16[2,32,16,1024]{3,2,0,1:T(8,128)(2,1)}, u32[]{:S(2)}, u32[]{:S(2)}) %all-to-all-start) | async-done | bytes 2097184 | tf_op jit(solution)/shard_map/all_to_all | solution.py:105
  68.8 2.3 fusion.62
  71.4 4.0 fusion.20
  77.2 38.8 %all_gather.15 = bf16[128,1024]{1,0:T(8,128)(2,1)S(1)} all-gather(bf16[16,1024]{1,0:T(8,128)(2,1)S(1)} %multiply_convert_fusion.3), channel_id=1, replica_groups=mesh['var'=32,'tok'=8] {'tok'}, dimensions={0}, use_global_device_ids=true | all-gather | bytes 294912 | tf_op jit(solution)/shard_map/all_gather | solution.py:118
  117.1 70.8 %all-gather.2.cloned.1.call-done = bf16[4096,2,128]{0,2,1:T(8,128)(2,1)} async-done(((bf16[128,2,128]{0,2,1:T(8,128)(2,1)}), bf16[4096,2,128]{0,2,1:T(8,128)(2,1)}) %all-gather.2.cloned.1.call-update) | async-done | bytes 2097168 | tf_op jit(solution)/shard_map/all_gather | solution.py:124
  188.0 11.4 %while.26 = (s32[]{:T(128)}, f32[128,2,64]{0,2,1:T(8,128)S(1)}, f32[2,128]{1,0:T(2,128)S(1)}, s32[2]{0:T(128)S(1)}, bf16[4096,2,128]{0,2,1:T(8,128)(2,1)}, /*ind...) while((s32[]{:T(128)}, f32[128,2,64]{0,2,1:T(8,128)S(1)}, ...), condition=%wide.region_5.6_spmd.clone, body=%wide.region_3.5_spmd.clone.sunk | while | flops 135823616 | bytes 5411022 | solution.py:155
  200.5 39.0 %all_gather.18 = bf16[128,1024]{1,0:T(8,128)(2,1)S(1)} all-gather(bf16[16,1024]{1,0:T(8,128)(2,1)S(1)} %copy-done.11), channel_id=1, replica_groups=mesh['var'=32,'tok'=8] {'tok'}, dimensions={0}, use_global_device_ids=true | all-gather | bytes 294912 | tf_op jit(solution)/shard_map/all_gather | solution.py:180
  239.5 40.3 %reduce-scatter.12.cloned.1.call-done = bf16[16,1024]{1,0:T(8,128)(2,1)} async-done(((bf16[128,1024]{1,0:T(8,128)(2,1)}), bf16[16,1024]{1,0:T(8,128)(2,1)}) %reduce-scatter.12.cloned.1.call-update) | async-done | bytes 32784 | tf_op jit(solution)/shard_map/reduce_scatter | solution.py:158
  281.0 38.8 %all_gather.17 = bf16[128,1024]{1,0:T(8,128)(2,1)S(1)} all-gather(bf16[16,1024]{1,0:T(8,128)(2,1)S(1)} %multiply_convert_fusion.2), channel_id=1, replica_groups=mesh['var'=32,'tok'=8] {'tok'}, dimensions={0}, use_global_device_ids=true | all-gather | bytes 294912 | tf_op jit(solution)/shard_map/all_gather | solution.py:166
  321.4 3.2 convolution_convert_fusion.2
  324.6 2.3 convolution_convert_fusion.3
  327.0 82.3 %reduce-scatter.16.cloned.1.call-done = bf16[16,1024]{1,0:T(8,128)(2,1)} async-done(((bf16[128,1024]{1,0:T(8,128)(2,1)}), bf16[16,1024]{1,0:T(8,128)(2,1)}) %reduce-scatter.16.cloned.1.call-update) | async-done | bytes 32784 | tf_op jit(solution)/shard_map/reduce_scatter | solution.py:187
  410.2 81.9 %reduce-scatter.14.cloned.1.call-done = bf16[16,1024]{1,0:T(8,128)(2,1)} async-done(((bf16[128,1024]{1,0:T(8,128)(2,1)}), bf16[16,1024]{1,0:T(8,128)(2,1)}) %reduce-scatter.14.cloned.1.call-update) | async-done | bytes 32784 | tf_op jit(solution)/shard_map/reduce_scatter | solution.py:171
  493.7 39.0 %all_gather.19 = bf16[128,1024]{1,0:T(8,128)(2,1)S(1)} all-gather(bf16[16,1024]{1,0:T(8,128)(2,1)S(1)} %fusion.60), channel_id=1, replica_groups=mesh['var'=32,'tok'=8] {'tok'}, dimensions={0}, use_global_device_ids=true | all-gather | bytes 294912 | tf_op jit(solution)/shard_map/all_gather | solution.py:199
  534.1 24.2 %while.27 = (s32[]{:T(128)}, f32[128,2,64]{0,2,1:T(8,128)S(1)}, bf16[2,2048,2,128]{1,3,2,0:T(8,128)(2,1)}, s32[2]{0:T(128)}, bf16[4096,2,128]{0,2,1:T(8,128)(2,1...) while((s32[]{:T(128)}, f32[128,2,64]{0,2,1:T(8,128)S(1)}, ...), condition=%wide.region_15.16_spmd.clone, body=%wide.region_14.15_spmd.clone.sunk | while | flops 341344256 | bytes 43780440 | solution.py:228
  542.0 2.2 fusion.171
  554.1 2.2 fusion.171
  558.3 3.9 copy.77
  562.4 145.2 %reduce-scatter.18.cloned.1.call-done = bf16[128,2,128]{2,0,1:T(8,128)(2,1)} async-done(((bf16[4096,2,128]{2,0,1:T(8,128)(2,1)}), bf16[128,2,128]{2,0,1:T(8,128)(2,1)}) %reduce-scatter.18.cloned.1.call-update) | async-done | bytes 65552 | tf_op jit(solution)/shard_map/reduce_scatter | solution.py:229
  707.7 2.0 fusion.24
  709.7 84.0 %reduce-scatter.20.cloned.1.call-done = bf16[16,1024]{1,0:T(8,128)(2,1)} async-done(((bf16[128,1024]{1,0:T(8,128)(2,1)}), bf16[16,1024]{1,0:T(8,128)(2,1)}) %reduce-scatter.20.cloned.1.call-update) | async-done | bytes 32784 | tf_op jit(solution)/shard_map/reduce_scatter | solution.py:239
  797.3 2.0 fusion.23
  799.2 3.1 fusion.33
  802.3 3.1 fusion.15
  805.4 4.8 fusion.19
  810.2 2.7 copy.83
  813.0 56.1 %all_to_all.30 = bf16[64,1,16,1024]{3,2,1,0:T(8,128)(2,1)S(1)} all-to-all(bf16[64,1,16,1024]{3,2,1,0:T(8,128)(2,1)S(1)} %copy.83), channel_id=1, replica_groups=mesh['var'=32,'tok'=8] {'var'}, dimensions={0} | all-to-all | bytes 4194304 | tf_op jit(solution)/shard_map/all_to_all | solution.py:252
  871.9 2.1 fusion.25
  875.4 74.6 %reduce-scatter.24.cloned.1.call-done = bf16[128,2]{1,0:T(8,128)(2,1)} async-done(((bf16[1024,2]{1,0:T(8,128)(2,1)}), bf16[128,2]{1,0:T(8,128)(2,1)}) %reduce-scatter.24.cloned.1.call-update) | async-done | bytes 528
  951.4 81.6 %reduce-scatter.22.cloned.1.call-done = bf16[128,128]{1,0:T(8,128)(2,1)} async-done(((bf16[1024,128]{1,0:T(8,128)(2,1)}), bf16[128,128]{1,0:T(8,128)(2,1)}) %reduce-scatter.22.cloned.1.call-update) | async-done | bytes 32784
  (155 shorter events, 54.8 us)
Async XLA Ops:
  7.2 69.1 %copy-start = (bf16[1024,1024]{1,0:T(8,128)(2,1)S(1)}, bf16[1024,1024]{1,0:T(8,128)(2,1)}, u32[]{:S(2)}) copy-start(bf16[1024,1024]{1,0:T(8,128)(2,1)} %param.23) | copy-start | bytes 6291460
  10.5 58.3 %all-to-all-start = ((bf16[2,32,16,1024]{3,2,0,1:T(8,128)(2,1)}), bf16[2,32,16,1024]{3,2,0,1:T(8,128)(2,1)}, u32[]{:S(2)}, u32[]{:S(2)}) async-start(bf16[2,32,16,1024]{3,2,0,1:T(8,128)(2,1)} %copy.70), calls=%async_computation | async-start | bytes 4194304 | tf_op jit(solution)/shard_map/all_to_all | solution.py:105
  20.6 4.1 copy-start.4
  20.6 48.2 %copy-start.13 = (bf16[16,1024]{1,0:T(8,128)(2,1)S(1)}, bf16[16,1024]{1,0:T(8,128)(2,1)}, u32[]{:S(2)}) copy-start(bf16[16,1024]{1,0:T(8,128)(2,1)} %param.21) | copy-start | bytes 98308
  20.6 167.3 %all-gather.2.cloned.1.call-start = ((), (), s32[]{:S(2)}) async-start(), calls=%async_computation.9 | async-start | bytes 2162688 | tf_op jit(solution)/shard_map/all_gather | solution.py:124
  71.3 4.2 copy-start.3
  75.5 1.6 copy-start.15
  76.2 39.8 %copy-start.6 = (bf16[3,1024,128]{1,2,0:T(8,128)(2,1)S(1)}, bf16[3,1024,128]{1,2,0:T(8,128)(2,1)}, u32[]{:S(2)}) copy-start(bf16[3,1024,128]{1,2,0:T(8,128)(2,1)} %copy.76) | copy-start | bytes 2359300
  76.8 111.1 %copy-start.18 = (f32[16]{0:T(128)}, f32[16]{0:T(128)S(1)}, u32[]{:S(2)}) copy-start(f32[16]{0:T(128)S(1)} %broadcast_multiply_fusion.1) | copy-start | bytes 196
  77.0 110.9 %copy-start.24 = (f32[16]{0:T(128)}, f32[16]{0:T(128)S(1)}, u32[]{:S(2)}) copy-start(f32[16]{0:T(128)S(1)} %multiply_reduce_fusion.5) | copy-start | bytes 196
  77.1 110.9 %copy-start.20 = (f32[16]{0:T(128)}, f32[16]{0:T(128)S(1)}, u32[]{:S(2)}) copy-start(f32[16]{0:T(128)S(1)} %fusion.70) | copy-start | bytes 196
  117.0 162.8 %reduce-scatter.12.cloned.1.call-start = ((), (), s32[]{:S(2)}) async-start(), calls=%async_computation.10 | async-start | bytes 294912 | tf_op jit(solution)/shard_map/reduce_scatter | solution.py:158
  187.9 11.5 %copy-start.9 = (bf16[128,1024]{1,0:T(8,128)(2,1)S(1)}, bf16[128,1024]{1,0:T(8,128)(2,1)}, u32[]{:S(2)}) copy-start(bf16[128,1024]{1,0:T(8,128)(2,1)} %param.28) | copy-start | bytes 786436
  187.9 12.5 %copy-start.11 = (bf16[16,1024]{1,0:T(8,128)(2,1)S(1)}, bf16[16,1024]{1,0:T(8,128)(2,1)}, u32[]{:S(2)}) copy-start(bf16[16,1024]{1,0:T(8,128)(2,1)} %param.31) | copy-start | bytes 98308
  187.9 93.0 %copy-start.16 = (f32[1024]{0:T(1024)S(1)}, f32[1024]{0:T(1024)}, u32[]{:S(2)}) copy-start(f32[1024]{0:T(1024)} %param.26) | copy-start | bytes 12292
  200.4 208.8 %reduce-scatter.16.cloned.1.call-start = ((), (), s32[]{:S(2)}) async-start(), calls=%async_computation.12 | async-start | bytes 294912 | tf_op jit(solution)/shard_map/reduce_scatter | solution.py:187
  324.5 167.5 %reduce-scatter.14.cloned.1.call-start = ((), (), s32[]{:S(2)}) async-start(), calls=%async_computation.11 | async-start | bytes 294912 | tf_op jit(solution)/shard_map/reduce_scatter | solution.py:171
  326.9 380.8 %reduce-scatter.18.cloned.1.call-start = ((), (), s32[]{:S(2)}) async-start(), calls=%async_computation.13 | async-start | bytes 2162688 | tf_op jit(solution)/shard_map/reduce_scatter | solution.py:229
  493.6 40.5 %copy-start.22 = (f32[16]{0:T(128)}, f32[16]{0:T(128)S(1)}, u32[]{:S(2)}) copy-start(f32[16]{0:T(128)S(1)} %negate_multiply_fusion.1) | copy-start | bytes 196
  538.0 1.4 copy-start.1
  542.0 2.7 copy-start.7
  554.1 2.7 copy-start.7
  562.2 145.5 %copy-start.5 = (bf16[3,1024,128]{2,1,0:T(8,128)(2,1)S(1)}, bf16[3,1024,128]{2,1,0:T(8,128)(2,1)}, u32[]{:S(2)}) copy-start(bf16[3,1024,128]{2,1,0:T(8,128)(2,1)} %param.27) | copy-start | bytes 2359300
  562.2 231.5 %copy-start.19 = (f32[16]{0:T(128)S(1)}, f32[16]{0:T(128)}, u32[]{:S(2)}) copy-start(f32[16]{0:T(128)} %copy-done.18) | copy-start | bytes 196
  562.2 232.5 %copy-start.25 = (f32[16]{0:T(128)S(1)}, f32[16]{0:T(128)}, u32[]{:S(2)}) copy-start(f32[16]{0:T(128)} %copy-done.24) | copy-start | bytes 196
  562.2 232.5 %copy-start.21 = (f32[16]{0:T(128)S(1)}, f32[16]{0:T(128)}, u32[]{:S(2)}) copy-start(f32[16]{0:T(128)} %copy-done.20) | copy-start | bytes 196
  562.2 233.5 %copy-start.12 = (bf16[16,1024]{1,0:T(8,128)(2,1)S(1)}, bf16[16,1024]{1,0:T(8,128)(2,1)}, u32[]{:S(2)}) copy-start(bf16[16,1024]{1,0:T(8,128)(2,1)} %param.31) | copy-start | bytes 98308
  562.2 233.5 %copy-start.23 = (f32[16]{0:T(128)S(1)}, f32[16]{0:T(128)}, u32[]{:S(2)}) copy-start(f32[16]{0:T(128)} %copy-done.22) | copy-start | bytes 196
  562.3 231.5 %reduce-scatter.20.cloned.1.call-start = ((), (), s32[]{:S(2)}) async-start(), calls=%async_computation.14 | async-start | bytes 294912 | tf_op jit(solution)/shard_map/reduce_scatter | solution.py:239
  709.7 240.3 %reduce-scatter.24.cloned.1.call-start = ((), (), s32[]{:S(2)}) async-start(), calls=%async_computation.16 | async-start | bytes 294912
  802.3 3.1 copy-start.14
  871.9 161.1 %reduce-scatter.22.cloned.1.call-start = ((), (), s32[]{:S(2)}) async-start(), calls=%async_computation.15 | async-start | bytes 294912
  (7 other events, 7.9 us)
Sparse Core Ops, SparseCore 0:
  117.1 70.7 all-gather.1
  200.6 79.2 reduce-scatter.11
  324.7 84.5 reduce-scatter.15
  413.0 79.0 reduce-scatter.13
  562.4 145.2 reduce-scatter.17
  711.4 82.3 reduce-scatter.19
  872.0 77.9 reduce-scatter.23
  953.8 79.0 reduce-scatter.21
where the time goes:
time: 1040 us
  waiting for transfers between devices  704 us (68%)
  blocking collectives  212 us (20%)
  matrix products  54.9 us (5%)
  local copies, waits for them, and re-layouts  35.3 us (3%)
  between operations  14.5 us (1%)
  starting transfers between devices  10.4 us (1%)
    unnamed x10, waiting for transfers between devices  156 us
    reduce_scatter x1, waiting for transfers between devices, local(): lax.psum_scatter(key_terms.reshape(seq, 2, local_width).astype(jnp.bfloat...  145 us
    reduce_scatter x1, waiting for transfers between devices, local(): lax.psum_scatter(jnp.einsum('nsc,sdc->nd', part, w_qkv, preferred_element...  84 us
    reduce_scatter x1, waiting for transfers between devices, local(): lax.psum_scatter(jnp.einsum('nf,df->nd', part, w_up, preferred_element_ty...  82.3 us
    reduce_scatter x1, waiting for transfers between devices, local(): lax.psum_scatter(jnp.dot(hidden, w_down, preferred_element_type=jnp.float...  81.9 us
    all_gather x1, waiting for transfers between devices, local(): keys_values = lax.all_gather(qkv[:, 1:], 'var', axis=0, tiled=True)  70.8 us
    all_to_all x1, blocking collectives, local(): lax.all_to_all(grad_tokens.reshape(var_local * var_count, 1, rows, width)...  56.1 us
    all_to_all x1, waiting for transfers between devices, local(): lax.all_to_all(embedded.reshape(var_local, var_count, rows, width), 'var'...  42.9 us
  transfers between devices with their start and end apart: 9, of which 9 were waited for; matrix products, arithmetic and copies ran while one was open for 1% of the time, Pallas kernels for 0%

commit v1 on v0

--- a/solution.py
+++ b/solution.py
@@ -15,52 +15,6 @@
 
 def smooth_gelu(values):
     return jax.nn.gelu(values, approximate=True)
-
-
-def pool_forward(embedded, agg_keys, agg_value, agg_out):
-    heads, width = agg_keys.shape
-    size = width // heads
-    scale = size ** (-0.5)
-    scores = (
-        jnp.einsum("vnd,hd->nhv", embedded, agg_keys, preferred_element_type=jnp.float32) * scale
-    )
-    expo = jnp.exp(scores)
-    probs = expo / jnp.sum(expo, axis=-1, keepdims=True)
-    probs_b = probs.astype(jnp.bfloat16)
-    pooled = jnp.einsum(
-        "nhv,vnd->nhd", probs_b, embedded, preferred_element_type=jnp.float32
-    ).astype(jnp.bfloat16)
-    value_three = agg_value.reshape(width, heads, size)
-    picked = jnp.einsum(
-        "nhd,dhe->nhe", pooled, value_three, preferred_element_type=jnp.float32
-    ).astype(jnp.bfloat16)
-    mixed = jnp.dot(picked.reshape(-1, width), agg_out, preferred_element_type=jnp.float32)
-    return (mixed, (probs, probs_b))
-
-
-def pool_backward(embedded, agg_keys, agg_value, agg_out, saved, grad_mixed):
-    probs, probs_b = saved
-    heads, width = agg_keys.shape
-    size = width // heads
-    scale = size ** (-0.5)
-    grad_picked = jnp.einsum(
-        "nk,dk->nd", grad_mixed, agg_out, preferred_element_type=jnp.float32
-    ).astype(jnp.bfloat16)
-    grad_picked = grad_picked.reshape(-1, heads, size)
-    value_three = agg_value.reshape(width, heads, size)
-    grad_pooled = jnp.einsum(
-        "nhe,dhe->nhd", grad_picked, value_three, preferred_element_type=jnp.float32
-    ).astype(jnp.bfloat16)
-    grad_pool = jnp.einsum(
-        "nhd,vnd->nhv", grad_pooled, embedded, preferred_element_type=jnp.float32
-    )
-    inner = jnp.sum(probs * grad_pool, axis=-1, keepdims=True)
-    grad_pool_scores = (probs * (grad_pool - inner) * scale).astype(jnp.bfloat16)
-    first = jnp.einsum("nhv,nhd->vnd", probs_b, grad_pooled, preferred_element_type=jnp.float32)
-    second = jnp.einsum(
-        "nhv,hd->vnd", grad_pool_scores, agg_keys, preferred_element_type=jnp.float32
-    )
-    return (first + second).astype(jnp.bfloat16)
 
 
 def score_block(query, key_block, value_block, grad_att, total, delta, scale):
@@ -100,17 +54,35 @@
     scale = size ** (-0.5)
     local_width = w_out.shape[0]
     local_heads = local_width // size
-    embedded = jnp.einsum("vpn,vpd->vnd", patches, embed_weight, preferred_element_type=jnp.float32)
-    embedded = (embedded + var_embed[:, None, :]).astype(jnp.bfloat16)
-    arrived = lax.all_to_all(
-        embedded.reshape(var_local, var_count, rows, width),
+    keyed = jnp.einsum("vpd,hd->vhp", embed_weight, agg_keys, preferred_element_type=jnp.float32)
+    var_b = var_embed.astype(jnp.bfloat16)
+    keyed_bias = jnp.einsum("vd,hd->vh", var_embed, agg_keys.astype(jnp.float32), precision="highest")
+    scores = jnp.einsum(
+        "vhp,vpn->vhn",
+        keyed.astype(jnp.bfloat16),
+        patches,
+        preferred_element_type=jnp.float32,
+    )
+    expo_pool = jnp.exp((scores + keyed_bias[:, :, None]) * scale)
+    pool_total = lax.psum(jnp.sum(expo_pool, axis=0), "var")
+    probs = expo_pool / pool_total
+    probs_b = probs.astype(jnp.bfloat16)
+    valued = jnp.einsum(
+        "vpd,dc->vpc", embed_weight, agg_value, preferred_element_type=jnp.float32
+    ).astype(jnp.bfloat16)
+    valued_bias = jnp.einsum("vd,dc->vc", var_b, agg_value, preferred_element_type=jnp.float32)
+    valued_tokens = (
+        jnp.einsum("vpn,vpc->vnc", patches, valued, preferred_element_type=jnp.float32)
+        + valued_bias[:, None, :]
+    )
+    wide = jnp.repeat(jnp.swapaxes(probs_b, 1, 2), size, axis=2).astype(jnp.float32)
+    picked = lax.psum_scatter(
+        jnp.sum(wide * valued_tokens, axis=0).astype(jnp.bfloat16),
         "var",
-        split_axis=1,
-        concat_axis=0,
-        tiled=True,
-    )
-    token_vars = arrived.reshape(var_local * var_count, rows, width)
-    mixed, saved = pool_forward(token_vars, agg_keys, agg_value, agg_out)
+        scatter_dimension=0,
+        tiled=True,
+    )
+    mixed = jnp.dot(picked, agg_out, preferred_element_type=jnp.float32)
     x_first = mixed + pos_embed.astype(jnp.float32)
     normed_first = layer_norm(x_first, norm_first).astype(jnp.bfloat16)
     qkv = jnp.einsum(
@@ -246,21 +218,41 @@
     ).astype(jnp.float32)
     _, first_back = jax.vjp(lambda inner: layer_norm(inner, norm_first), x_first)
     grad_first = grad_second + first_back(grad_normed_first)[0]
-    grad_tokens = pool_backward(
-        token_vars, agg_keys, agg_value, agg_out, saved, grad_first.astype(jnp.bfloat16)
-    )
-    returned = lax.all_to_all(
-        grad_tokens.reshape(var_local * var_count, 1, rows, width),
-        "var",
-        split_axis=0,
-        concat_axis=1,
-        tiled=True,
-    )
-    grad_embedded = returned.reshape(var_local, span, width)
+    grad_picked = jnp.einsum(
+        "nk,dk->nd",
+        grad_first.astype(jnp.bfloat16),
+        agg_out,
+        preferred_element_type=jnp.float32,
+    ).astype(jnp.bfloat16)
+    grad_picked_all = lax.all_gather(grad_picked, "var", axis=0, tiled=True)
+    picked_all = lax.all_gather(picked, "var", axis=0, tiled=True)
+    gp = grad_picked_all.astype(jnp.float32)
+    inner = jnp.sum((gp * picked_all.astype(jnp.float32)).reshape(span, heads, size), axis=2).T
+    grad_pool = jnp.swapaxes(
+        jnp.sum((gp[None] * valued_tokens).reshape(var_local, span, heads, size), axis=3), 1, 2
+    )
+    grad_pool_scores = (probs * (grad_pool - inner[None]) * scale).astype(jnp.bfloat16)
+    weighted = (wide * gp[None]).astype(jnp.bfloat16)
+    value_term = jnp.einsum(
+        "vpn,vnc->vpc", patches, weighted, preferred_element_type=jnp.float32
+    ).astype(jnp.bfloat16)
+    key_term = jnp.einsum(
+        "vpn,vhn->vph", patches, grad_pool_scores, preferred_element_type=jnp.float32
+    ).astype(jnp.bfloat16)
     embed_term = jnp.einsum(
-        "vpn,vnd->vpd", patches, grad_embedded, preferred_element_type=jnp.float32
-    )
-    var_term = jnp.sum(grad_embedded, axis=1, dtype=jnp.float32)
+        "vpc,dc->vpd", value_term, agg_value, preferred_element_type=jnp.float32
+    ) + jnp.einsum("vph,hd->vpd", key_term, agg_keys, preferred_element_type=jnp.float32)
+    var_term = jnp.einsum(
+        "vc,dc->vd",
+        jnp.sum(weighted, axis=1, dtype=jnp.float32).astype(jnp.bfloat16),
+        agg_value,
+        preferred_element_type=jnp.float32,
+    ) + jnp.einsum(
+        "vh,hd->vd",
+        jnp.sum(grad_pool_scores, axis=2, dtype=jnp.float32).astype(jnp.bfloat16),
+        agg_keys,
+        preferred_element_type=jnp.float32,
+    )
     grad_embed, grad_var_embed = (
         lax.psum_scatter(
             embed_term.astype(jnp.bfloat16), "tok", scatter_dimension=2, tiled=True

time: 1040 us -> 1320 us (1.27)
  waiting for transfers between devices: 704 us -> 915 us
  blocking collectives: 212 us -> 290 us
    reduce_scatter x0 -> x1, waiting for transfers between devices: none -> 142 us  [local(): lax.psum_scatter(jnp.sum(wide * valued_tokens, axis=0).astype(jnp.bfloat1...]
    psum x0 -> x1, blocking collectives: none -> 135 us  [local(): pool_total = lax.psum(jnp.sum(expo_pool, axis=0), 'var')]
    all_gather x0 -> x2, waiting for transfers between devices: none -> 107 us  [the longest x1 56.7 us: local(): grad_picked_all = lax.all_gather(grad_picked, 'var', axis=0, tiled=True)]
    all_to_all x1 -> x0, blocking collectives: 56.1 us -> none  [local(): lax.all_to_all(grad_tokens.reshape(var_local * var_count, 1, rows, width)...]
    all_to_all x1 -> x0, waiting for transfers between devices: 42.9 us -> none  [local(): lax.all_to_all(embedded.reshape(var_local, var_count, rows, width), 'var'...]
    unnamed x10 -> x13, waiting for transfers between devices: 156 us -> 161 us
  transfers between devices with their start and end apart: 9 -> 11, of which waited for: 9 -> 11; matrix products, arithmetic and copies ran while one was open for 1% -> 1% of each run, Pallas kernels for 0% -> 0%
where the time goes in v1:
time: 1320 us
  waiting for transfers between devices  915 us (69%)
  blocking collectives  290 us (22%)
  matrix products  45 us (3%)
  local copies, waits for them, and re-layouts  34.1 us (3%)
  other arithmetic  19.4 us (1%)
  between operations  14.4 us (1%)
    unnamed x13, waiting for transfers between devices  161 us
    reduce_scatter x1, waiting for transfers between devices, local(): lax.psum_scatter(key_terms.reshape(seq, 2, local_width).astype(jnp.bfloat...  145 us
    reduce_scatter x1, waiting for transfers between devices, local(): lax.psum_scatter(jnp.sum(wide * valued_tokens, axis=0).astype(jnp.bfloat1...  142 us
    psum x1, blocking collectives, local(): pool_total = lax.psum(jnp.sum(expo_pool, axis=0), 'var')  135 us
    reduce_scatter x1, waiting for transfers between devices, local(): lax.psum_scatter(jnp.einsum('nsc,sdc->nd', part, w_qkv, preferred_element...  84.6 us
    reduce_scatter x1, waiting for transfers between devices, local(): lax.psum_scatter(jnp.dot(hidden, w_down, preferred_element_type=jnp.float...  82.4 us
    reduce_scatter x1, waiting for transfers between devices, local(): lax.psum_scatter(jnp.einsum('nf,df->nd', part, w_up, preferred_element_ty...  82.2 us
    all_gather x1, waiting for transfers between devices, local(): keys_values = lax.all_gather(qkv[:, 1:], 'var', axis=0, tiled=True)  71.2 us
  transfers between devices with their start and end apart: 11, of which 11 were waited for; matrix products, arithmetic and copies ran while one was open for 1% of the time, Pallas kernels for 0%

profile of v1, /device:TPU:1, one launch (start us, length us, event | category | flops | bytes accessed | tf_op | source)
XLA Modules:
  0.0 1321.1 jit_solution(17436313794173975864)
XLA Ops:
  10.4 134.7 %psum.7 = f32[16,512]{1,0:T(8,128)S(1)} all-reduce(f32[16,512]{1,0:T(8,128)S(1)} %get-tuple-element.182), channel_id=1, replica_groups=mesh['var'=32,'tok'=8] {'var'}, use_global_device_ids=true, to_apply=%region_1.0 | all-reduce | flops 8192 | bytes 65536 | tf_op jit(solution)/shard_map/psum | solution.py:67
  145.1 4.2 fusion.13
  152.1 142.2 %reduce-scatter.13.cloned.1.call-done = bf16[16,1024]{1,0:T(8,128)(2,1)} async-done(((bf16[512,1024]{1,0:T(8,128)(2,1)}), bf16[16,1024]{1,0:T(8,128)(2,1)}) %reduce-scatter.13.cloned.1.call-update) | async-done | bytes 32784 | tf_op jit(solution)/shard_map/reduce_scatter | solution.py:79
  294.3 2.1 fusion.93
  296.7 38.5 %all_gather.21 = bf16[128,1024]{1,0:T(8,128)(2,1)S(1)} all-gather(bf16[16,1024]{1,0:T(8,128)(2,1)S(1)} %multiply_convert_fusion.4), channel_id=1, replica_groups=mesh['var'=32,'tok'=8] {'tok'}, dimensions={0}, use_global_device_ids=true | all-gather | bytes 294912 | tf_op jit(solution)/shard_map/all_gather | solution.py:90
  336.3 71.2 %all-gather.4.cloned.1.call-done = bf16[4096,2,128]{0,2,1:T(8,128)(2,1)} async-done(((bf16[128,2,128]{0,2,1:T(8,128)(2,1)}), bf16[4096,2,128]{0,2,1:T(8,128)(2,1)}) %all-gather.4.cloned.1.call-update) | async-done | bytes 2097168 | tf_op jit(solution)/shard_map/all_gather | solution.py:96
  407.6 11.4 while.26
  420.1 39.1 %all_gather.24 = bf16[128,1024]{1,0:T(8,128)(2,1)S(1)} all-gather(bf16[16,1024]{1,0:T(8,128)(2,1)S(1)} %copy-done.16), channel_id=1, replica_groups=mesh['var'=32,'tok'=8] {'tok'}, dimensions={0}, use_global_device_ids=true | all-gather | bytes 294912 | tf_op jit(solution)/shard_map/all_gather | solution.py:152
  459.2 40.1 %reduce-scatter.15.cloned.1.call-done = bf16[16,1024]{1,0:T(8,128)(2,1)} async-done(((bf16[128,1024]{1,0:T(8,128)(2,1)}), bf16[16,1024]{1,0:T(8,128)(2,1)}) %reduce-scatter.15.cloned.1.call-update) | async-done | bytes 32784 | tf_op jit(solution)/shard_map/reduce_scatter | solution.py:130
  500.5 38.6 %all_gather.23 = bf16[128,1024]{1,0:T(8,128)(2,1)S(1)} all-gather(bf16[16,1024]{1,0:T(8,128)(2,1)S(1)} %multiply_convert_fusion.3), channel_id=1, replica_groups=mesh['var'=32,'tok'=8] {'tok'}, dimensions={0}, use_global_device_ids=true | all-gather | bytes 294912 | tf_op jit(solution)/shard_map/all_gather | solution.py:138
  540.7 3.2 convolution_convert_fusion.1
  543.9 2.3 convolution_convert_fusion.2
  546.3 82.2 %reduce-scatter.19.cloned.1.call-done = bf16[16,1024]{1,0:T(8,128)(2,1)} async-done(((bf16[128,1024]{1,0:T(8,128)(2,1)}), bf16[16,1024]{1,0:T(8,128)(2,1)}) %reduce-scatter.19.cloned.1.call-update) | async-done | bytes 32784 | tf_op jit(solution)/shard_map/reduce_scatter | solution.py:159
  629.5 82.4 %reduce-scatter.17.cloned.1.call-done = bf16[16,1024]{1,0:T(8,128)(2,1)} async-done(((bf16[128,1024]{1,0:T(8,128)(2,1)}), bf16[16,1024]{1,0:T(8,128)(2,1)}) %reduce-scatter.17.cloned.1.call-update) | async-done | bytes 32784 | tf_op jit(solution)/shard_map/reduce_scatter | solution.py:143
  713.5 38.8 %all_gather.25 = bf16[128,1024]{1,0:T(8,128)(2,1)S(1)} all-gather(bf16[16,1024]{1,0:T(8,128)(2,1)S(1)} %fusion.59), channel_id=1, replica_groups=mesh['var'=32,'tok'=8] {'tok'}, dimensions={0}, use_global_device_ids=true | all-gather | bytes 294912 | tf_op jit(solution)/shard_map/all_gather | solution.py:171
  753.7 24.6 %while.27 = (s32[]{:T(128)}, f32[128,2,64]{0,2,1:T(8,128)S(1)}, bf16[2,2048,2,128]{1,3,2,0:T(8,128)(2,1)}, s32[2]{0:T(128)}, bf16[4096,2,128]{0,2,1:T(8,128)(2,1...) while((s32[]{:T(128)}, f32[128,2,64]{0,2,1:T(8,128)S(1)}, ...), condition=%wide.region_18.19_spmd.clone, body=%wide.region_17.18_spmd.clone.sunk | while | flops 341344256 | bytes 43780440 | solution.py:200
  761.8 2.2 fusion.186
  774.1 2.2 fusion.186
  778.3 3.9 copy.33
  782.5 145.2 %reduce-scatter.21.cloned.1.call-done = bf16[128,2,128]{2,0,1:T(8,128)(2,1)} async-done(((bf16[4096,2,128]{2,0,1:T(8,128)(2,1)}), bf16[128,2,128]{2,0,1:T(8,128)(2,1)}) %reduce-scatter.21.cloned.1.call-update) | async-done | bytes 65552 | tf_op jit(solution)/shard_map/reduce_scatter | solution.py:201
  929.6 84.6 %reduce-scatter.23.cloned.1.call-done = bf16[16,1024]{1,0:T(8,128)(2,1)} async-done(((bf16[128,1024]{1,0:T(8,128)(2,1)}), bf16[16,1024]{1,0:T(8,128)(2,1)}) %reduce-scatter.23.cloned.1.call-update) | async-done | bytes 32784 | tf_op jit(solution)/shard_map/reduce_scatter | solution.py:211
  1016.2 2.9 convolution_convert_fusion.4
  1020.1 56.7 %all-gather.6.cloned.1.call-done = bf16[512,1024]{1,0:T(8,128)(2,1)} async-done(((bf16[16,1024]{1,0:T(8,128)(2,1)}), bf16[512,1024]{1,0:T(8,128)(2,1)}) %all-gather.6.cloned.1.call-update) | async-done | bytes 1048592 | tf_op jit(solution)/shard_map/all_gather | solution.py:227
  1076.9 2.6 copy.35
  1079.4 3.3 fusion.14
  1082.7 3.9 fusion.16
  1086.7 49.8 %all-gather.8.cloned.1.call-done = bf16[512,1024]{1,0:T(8,128)(2,1)} async-done(((bf16[16,1024]{1,0:T(8,128)(2,1)}), bf16[512,1024]{1,0:T(8,128)(2,1)}) %all-gather.8.cloned.1.call-update) | async-done | bytes 1048592 | tf_op jit(solution)/shard_map/all_gather | solution.py:228
  1136.5 2.9 convert_multiply_fusion
  1139.5 2.9 copy.37
  1144.6 3.0 bitcast_reduce_fusion
  1151.9 77.6 %reduce-scatter.27.cloned.1.call-done = bf16[128,2]{1,0:T(8,128)(2,1)} async-done(((bf16[1024,2]{1,0:T(8,128)(2,1)}), bf16[128,2]{1,0:T(8,128)(2,1)}) %reduce-scatter.27.cloned.1.call-update) | async-done | bytes 528
  1230.9 82.0 %reduce-scatter.25.cloned.1.call-done = bf16[128,128]{1,0:T(8,128)(2,1)} async-done(((bf16[1024,128]{1,0:T(8,128)(2,1)}), bf16[128,128]{1,0:T(8,128)(2,1)}) %reduce-scatter.25.cloned.1.call-update) | async-done | bytes 32784
  (178 shorter events, 58.3 us)
Async XLA Ops:
  7.2 2.8 copy-start.10
  7.2 287.0 %reduce-scatter.13.cloned.1.call-start = ((), (), s32[]{:S(2)}) async-start(), calls=%async_computation.8 | async-start | bytes 1081344 | tf_op jit(solution)/shard_map/reduce_scatter | solution.py:79
  10.4 134.7 %copy-start.14 = (f32[2,16,512]{2,1,0:T(8,128)}, f32[2,16,512]{2,1,0:T(8,128)S(1)}, u32[]{:S(2)}) copy-start(f32[2,16,512]{2,1,0:T(8,128)S(1)} %get-tuple-element.183) | copy-start | bytes 196612
  145.0 4.2 copy-start.18
  149.2 145.0 %copy-start.24 = (bf16[16,1024]{1,0:T(8,128)(2,1)S(1)}, bf16[16,1024]{1,0:T(8,128)(2,1)}, u32[]{:S(2)}) copy-start(bf16[16,1024]{1,0:T(8,128)(2,1)} %param.24) | copy-start | bytes 98308
  150.6 146.0 %copy-start.22 = (f32[1024]{0:T(1024)S(1)}, f32[1024]{0:T(1024)}, u32[]{:S(2)}) copy-start(f32[1024]{0:T(1024)} %param.25) | copy-start | bytes 12292
  150.6 256.9 %all-gather.4.cloned.1.call-start = ((), (), s32[]{:S(2)}) async-start(), calls=%async_computation.9 | async-start | bytes 2162688 | tf_op jit(solution)/shard_map/all_gather | solution.py:96
  296.4 39.9 %copy-start.25 = (f32[16]{0:T(128)}, f32[16]{0:T(128)S(1)}, u32[]{:S(2)}) copy-start(f32[16]{0:T(128)S(1)} %broadcast_multiply_fusion.1) | copy-start | bytes 196
  296.6 39.7 %copy-start.32 = (f32[16]{0:T(128)}, f32[16]{0:T(128)S(1)}, u32[]{:S(2)}) copy-start(f32[16]{0:T(128)S(1)} %multiply_reduce_fusion.4) | copy-start | bytes 196
  296.6 39.7 %copy-start.28 = (f32[16]{0:T(128)}, f32[16]{0:T(128)S(1)}, u32[]{:S(2)}) copy-start(f32[16]{0:T(128)S(1)} %fusion.69) | copy-start | bytes 196
  336.2 163.1 %reduce-scatter.15.cloned.1.call-start = ((), (), s32[]{:S(2)}) async-start(), calls=%async_computation.10 | async-start | bytes 294912 | tf_op jit(solution)/shard_map/reduce_scatter | solution.py:130
  407.5 11.5 copy-start.11
  407.6 12.5 copy-start.16
  407.6 92.9 %copy-start.23 = (f32[1024]{0:T(1024)S(1)}, f32[1024]{0:T(1024)}, u32[]{:S(2)}) copy-start(f32[1024]{0:T(1024)} %param.26) | copy-start | bytes 12292
  420.0 208.5 %reduce-scatter.19.cloned.1.call-start = ((), (), s32[]{:S(2)}) async-start(), calls=%async_computation.12 | async-start | bytes 294912 | tf_op jit(solution)/shard_map/reduce_scatter | solution.py:159
  543.9 168.0 %reduce-scatter.17.cloned.1.call-start = ((), (), s32[]{:S(2)}) async-start(), calls=%async_computation.11 | async-start | bytes 294912 | tf_op jit(solution)/shard_map/reduce_scatter | solution.py:143
  546.2 381.4 %reduce-scatter.21.cloned.1.call-start = ((), (), s32[]{:S(2)}) async-start(), calls=%async_computation.13 | async-start | bytes 2162688 | tf_op jit(solution)/shard_map/reduce_scatter | solution.py:201
  713.4 40.3 %copy-start.12 = (f32[16,1024]{1,0:T(8,128)}, f32[16,1024]{1,0:T(8,128)S(1)}, u32[]{:S(2)}) copy-start(f32[16,1024]{1,0:T(8,128)S(1)} %get-tuple-element.172) | copy-start | bytes 196612
  713.4 40.3 %copy-start.30 = (f32[16]{0:T(128)}, f32[16]{0:T(128)S(1)}, u32[]{:S(2)}) copy-start(f32[16]{0:T(128)S(1)} %negate_multiply_fusion.1) | copy-start | bytes 196
  782.2 145.4 %copy-start.5 = (bf16[3,1024,128]{2,1,0:T(8,128)(2,1)S(1)}, bf16[3,1024,128]{2,1,0:T(8,128)(2,1)}, u32[]{:S(2)}) copy-start(bf16[3,1024,128]{2,1,0:T(8,128)(2,1)} %param.27) | copy-start | bytes 2359300
  782.2 232.1 %copy-start.26 = (f32[16]{0:T(128)S(1)}, f32[16]{0:T(128)}, u32[]{:S(2)}) copy-start(f32[16]{0:T(128)} %copy-done.25) | copy-start | bytes 196
  782.2 233.0 %copy-start.33 = (f32[16]{0:T(128)S(1)}, f32[16]{0:T(128)}, u32[]{:S(2)}) copy-start(f32[16]{0:T(128)} %copy-done.32) | copy-start | bytes 196
  782.2 233.0 %copy-start.29 = (f32[16]{0:T(128)S(1)}, f32[16]{0:T(128)}, u32[]{:S(2)}) copy-start(f32[16]{0:T(128)} %copy-done.28) | copy-start | bytes 196
  782.2 234.0 %copy-start.13 = (f32[16,1024]{1,0:T(8,128)S(1)}, f32[16,1024]{1,0:T(8,128)}, u32[]{:S(2)}) copy-start(f32[16,1024]{1,0:T(8,128)} %copy-done.12) | copy-start | bytes 196612
  782.2 234.0 %copy-start.17 = (bf16[16,1024]{1,0:T(8,128)(2,1)S(1)}, bf16[16,1024]{1,0:T(8,128)(2,1)}, u32[]{:S(2)}) copy-start(bf16[16,1024]{1,0:T(8,128)(2,1)} %param.31) | copy-start | bytes 98308
  782.2 234.0 %copy-start.31 = (f32[16]{0:T(128)S(1)}, f32[16]{0:T(128)}, u32[]{:S(2)}) copy-start(f32[16]{0:T(128)} %copy-done.30) | copy-start | bytes 196
  782.3 232.0 %reduce-scatter.23.cloned.1.call-start = ((), (), s32[]{:S(2)}) async-start(), calls=%async_computation.14 | async-start | bytes 294912 | tf_op jit(solution)/shard_map/reduce_scatter | solution.py:211
  929.6 147.3 %all-gather.6.cloned.1.call-start = ((), (), s32[]{:S(2)}) async-start(), calls=%async_computation.15 | async-start | bytes 1081344 | tf_op jit(solution)/shard_map/all_gather | solution.py:227
  1019.2 117.4 %all-gather.8.cloned.1.call-start = ((), (), s32[]{:S(2)}) async-start(), calls=%async_computation.16 | async-start | bytes 1081344 | tf_op jit(solution)/shard_map/all_gather | solution.py:228
  1019.9 209.6 %reduce-scatter.27.cloned.1.call-start = ((), (), s32[]{:S(2)}) async-start(), calls=%async_computation.18 | async-start | bytes 294912
  1082.7 53.8 %copy-start.4 = (bf16[512,1024]{1,0:T(8,128)(2,1)S(1)}, bf16[512,1024]{1,0:T(8,128)(2,1)}, u32[]{:S(2)}) copy-start(bf16[512,1024]{1,0:T(8,128)(2,1)} %all-gather.6.cloned.1.call-done) | copy-start | bytes 3145732
  1150.1 162.9 %reduce-scatter.25.cloned.1.call-start = ((), (), s32[]{:S(2)}) async-start(), calls=%async_computation.17 | async-start | bytes 294912
  (17 other events, 30.6 us)
Sparse Core Ops, SparseCore 0:
  150.7 143.4 reduce-scatter.12
  336.3 71.1 all-gather.3
  420.1 79.1 reduce-scatter.14
  544.0 84.5 reduce-scatter.18
  632.7 79.0 reduce-scatter.16
  782.4 145.1 reduce-scatter.20
  932.0 82.2 reduce-scatter.22
  1019.3 57.5 all-gather.5
  1078.7 57.7 all-gather.7
  1150.2 79.2 reduce-scatter.26
  1233.9 79.0 reduce-scatter.24

commit v2 on v1

v2 whole, which is shorter than its diff:
```python
import jax
import jax.numpy as jnp
from jax import lax
from jax.experimental import pallas as pl
from jax.experimental.pallas import tpu as pltpu
from jax.sharding import PartitionSpec as P

EPS = 1e-05
MESH = pl.DeviceIdType.MESH
BF = jnp.bfloat16
F32 = jnp.float32

NZ, NX, NC, NY, NH = 4, 4, 2, 4, 2
ROWS, WIDTH, HEADS, SIZE, PIX = 16, 1024, 16, 64, 64
SPAN = 512
EXT = 80
GWIDTH = WIDTH + 128
LINKS = 160
SCALE = SIZE ** (-0.5)


def mm(a, b):
    return lax.dot_general(a, b, (((1,), (0,)), ((), ())), preferred_element_type=F32)


def mm_nt(a, b):
    return lax.dot_general(a, b, (((1,), (1,)), ((), ())), preferred_element_type=F32)


def norm_parts(values):
    mean = jnp.mean(values, axis=-1, keepdims=True)
    centred = values - mean
    spread = jnp.mean(centred * centred, axis=-1, keepdims=True)
    rstd = lax.rsqrt(spread + EPS)
    return centred * rstd, rstd


def norm_back(grad, hat, rstd, gain):
    inner = grad * gain
    first = jnp.mean(inner, axis=-1, keepdims=True)
    second = jnp.mean(inner * hat, axis=-1, keepdims=True)
    return rstd * (inner - first - hat * second)


def gelu_both(values):
    c = 0.7978845608028654
    a = 0.044715
    square = values * values
    t = jnp.tanh(c * values * (1.0 + a * square))
    half = 0.5 * (1.0 + t)
    slope = half + 0.5 * values * (1.0 - t * t) * c * (1.0 + 3.0 * a * square)
    return values * half, slope


SCRATCH = dict(
    px=((2, EXT, SPAN), BF),
    wx=((128, WIDTH), BF),
    akey=((16, WIDTH), BF),
    vemb=((2, WIDTH), F32),
    aval=((WIDTH, WIDTH), BF),
    aout=((WIDTH, WIDTH), BF),
    posv=((ROWS, WIDTH), BF),
    g1=((1, WIDTH), F32),
    g2=((1, WIDTH), F32),
    wq=((WIDTH, 384), BF),
    wo=((128, WIDTH), BF),
    wu=((WIDTH, 512), BF),
    wd=((512, WIDTH), BF),
    tsend=((2, 16, SPAN), BF),
    trecv=((10, 16, SPAN), BF),
    town=((16, SPAN), F32),
    expo=((32, SPAN), F32),
    ub=((2, 128, WIDTH), BF),
    ubias=((16, WIDTH), F32),
    ptl=((NZ, NX, 32, 128), BF),
    prl=((NZ, NX, 32, 128), F32),
    spread=((2, 128, WIDTH), BF),
    vals=((2, NZ, NX, 32, WIDTH), BF),
    part=((NZ, NX, NC, ROWS, WIDTH), BF),
    rc1=((NX, NZ, ROWS, WIDTH), BF),
    s1=((NX - 1, NZ, ROWS, WIDTH), BF),
    rm1=((2, NZ // 2, ROWS, WIDTH), BF),
    rx1=((2, NZ, ROWS, WIDTH), BF),
    own1=((NZ, ROWS, WIDTH), F32),
    s2=((NZ - 1, ROWS, WIDTH), BF),
    rz1=((NZ - 1, ROWS, WIDTH), BF),
    picked=((ROWS, WIDTH), F32),
    xh1=((ROWS, WIDTH), F32),
    xh2=((NH, ROWS, WIDTH), F32),
    xa=((NH, ROWS, WIDTH), F32),
    xb=((NH, ROWS, WIDTH), F32),
    gsec=((NH, ROWS, WIDTH), F32),
    xnear=((ROWS, WIDTH), BF),
    xfar=((ROWS, WIDTH), BF),
    bsz=((2, NH, ROWS, WIDTH), BF),
    brz=((2, NH, ROWS, WIDTH), BF),
    nf1=((NY, NH, ROWS, WIDTH), BF),
    cot=((NY, NH, ROWS, WIDTH), BF),
    nf2=((NY, NH, ROWS, WIDTH), BF),
    gsa=((NY, NH, ROWS, WIDTH), BF),
    tsrc=((4, NY, NH, ROWS, WIDTH), BF),
    try_=((4, NY - 1, NH, ROWS, WIDTH), BF),
    tsz=((4, ROWS, WIDTH), BF),
    trz=((4, ROWS, WIDTH), BF),
    fsrc=((NY, NH, 2 * EXT, 128), BF),
    fry=((NY - 1, NH, 2 * EXT, 128), BF),
    fsz=((2 * EXT, 128), BF),
    frz=((2 * EXT, 128), BF),
    qs=((256, 128), BF),
    kvb=((NZ, NX, NC, 128, 256), BF),
    es=((NX, NZ, 256, 256), BF),
    numt=((128, 256), F32),
    tot=((8, 256), F32),
    inv=((128, 128), F32),
    att=((128, 128), F32),
    gb=((256, 128), BF),
    dp=((NZ, NX, NC, 128, 256), BF),
    rc2=((NX, NZ, 128, 256), BF),
    s1b=((NX - 1, NZ, 128, 256), BF),
    rm2=((2, NZ // 2, 128, 256), BF),
    rx2=((2, NZ, 128, 256), BF),
    own2=((NZ, 128, 256), F32),
    s2b=((NZ - 1, 128, 256), BF),
    rz2=((NZ - 1, 128, 256), BF),
    gpre=((128, 512), BF),
    hid=((128, 512), BF),
    gpb=((NZ, NX, NC, ROWS, GWIDTH), BF),
    zs=((2, NZ, NX, 32, WIDTH), BF),
    gps=((NZ, NX, 32, 128), BF),
    kext=((128, WIDTH), BF),
)


ARGS = (
    "patches",
    "embed",
    "var_e",
    "keys",
    "a_val",
    "a_out",
    "pos",
    "n1",
    "n2",
    "wqkv",
    "w_out",
    "w_up",
    "w_down",
    "cotangent",
)
OUTS = ("out_ref", "sum_ref")


class Refs:
    pass


def kernel(*refs):
    names = ARGS + OUTS + tuple(SCRATCH)
    s = Refs()
    for name, ref in zip(names, refs):
        setattr(s, name, ref)
    send_sems, recv_sems, load_sems = refs[len(names) :]

    v = lax.axis_index("var")
    t = lax.axis_index("tok")
    c = lax.rem(v, 2)
    x = lax.rem(lax.div(v, 2), 4)
    z = lax.div(v, 8)
    y = lax.div(t, 2)
    h = lax.rem(t, 2)

    def turn(i, k):
        return lax.rem(i + k, 4)

    def dev(zz=None, xx=None, cc=None, yy=None, hh=None):
        zz = z if zz is None else zz
        xx = x if xx is None else xx
        cc = c if cc is None else cc
        yy = y if yy is None else yy
        hh = h if hh is None else hh
        return ((zz * 4 + xx) * 2 + cc, yy * 2 + hh)

    sibling = dev(cc=1 - c)
    partner = dev(hh=1 - h)
    started = []

    def send(src, dst, device):
        index = len(started)
        copy = pltpu.make_async_remote_copy(
            src_ref=src,
            dst_ref=dst,
            send_sem=send_sems.at[index],
            recv_sem=recv_sems.at[index],
            device_id=device,
            device_id_type=MESH,
        )
        copy.start()
        started.append(copy)
        return copy

    loads = []

    def load(src, dst):
        copy = pltpu.make_async_copy(src, dst, load_sems.at[len(loads)])
        copy.start()
        loads.append(copy)
        return copy

    l_first = [
        load(s.keys, s.akey),
        load(s.embed, s.wx),
        load(s.patches.at[0], s.px.at[0, pl.ds(0, PIX)]),
        load(s.patches.at[1], s.px.at[1, pl.ds(0, PIX)]),
        load(s.var_e, s.vemb),
    ]
    l_val = load(s.a_val, s.aval)
    l_cot = load(s.cotangent, s.cot.at[y, h])
    l_mix = [load(s.a_out, s.aout), load(s.pos, s.posv), load(s.n1, s.g1)]
    l_qkv = [load(s.wqkv.at[i], s.wq.at[:, pl.ds(i * 128, 128)]) for i in range(3)]
    l_wo = load(s.w_out, s.wo)
    l_mlp = [load(s.n2, s.g2), load(s.w_up, s.wu), load(s.w_down, s.wd)]

    peers = [sibling, partner]
    for k in (1, 2, 3):
        peers += [dev(zz=turn(z, k)), dev(xx=turn(x, k)), dev(yy=turn(y, k))]
        peers += [dev(xx=turn(x, k), cc=1 - c)]
    barrier = pltpu.get_barrier_semaphore()
    for peer in peers:
        pl.semaphore_signal(barrier, inc=1, device_id=peer, device_id_type=MESH)

    lane_head = lax.broadcasted_iota(jnp.int32, (128, WIDTH), 1) // SIZE
    row = lax.broadcasted_iota(jnp.int32, (128, WIDTH), 0)
    for i in range(2):
        s.spread[i] = jnp.where(row == lane_head + i * 16, 1.0, 0.0).astype(BF)
        ones = lax.broadcasted_iota(jnp.int32, (EXT - PIX, SPAN), 0)
        s.px[i, PIX:EXT] = jnp.where(ones == 0, 1.0, 0.0).astype(BF)

    for copy in l_first:
        copy.wait()
    key_t = mm_nt(s.akey[...], s.wx[...])
    both = jnp.concatenate([key_t, key_t], axis=0)
    rows32 = lax.broadcasted_iota(jnp.int32, (32, 128), 0) // 16
    lanes32 = lax.broadcasted_iota(jnp.int32, (32, 128), 1) // PIX
    both = jnp.where(rows32 == lanes32, both, 0.0).astype(BF)
    rows16 = lax.broadcasted_iota(jnp.int32, (16, WIDTH), 0)
    var_rows = jnp.where(
        rows16 == 0, s.vemb[0:1, :], jnp.where(rows16 == 1, s.vemb[1:2, :], 0.0)
    ).astype(BF)
    key_bias = mm_nt(s.akey[...], var_rows)
    bias32 = jnp.concatenate([key_bias[:, 0:1], key_bias[:, 1:2]], axis=0)
    pixels = jnp.concatenate([s.px[0, 0:PIX], s.px[1, 0:PIX]], axis=0)
    expo = jnp.exp((mm(both, pixels) + bias32) * SCALE)
    s.expo[...] = expo
    s.town[...] = expo[0:16] + expo[16:32]
    s.tsend[0] = s.town[...].astype(BF)
    s.ptl[...] = jnp.transpose(pixels).reshape(NZ, NX, 32, 128)

    pl.semaphore_wait(barrier, len(peers))
    t_near = [send(s.tsend.at[0], s.trecv.at[0], sibling)]
    for k in (2, 1, 3):
        t_near.append(send(s.tsend.at[0], s.trecv.at[2 * k - 1], dev(xx=turn(x, k))))
        t_near.append(send(s.tsend.at[0], s.trecv.at[2 * k], dev(xx=turn(x, k), cc=1 - c)))

    def gather_tok_start(buf):
        first = send(buf.at[y, h], buf.at[y, h], partner)
        direct = [
            send(buf.at[y, h], buf.at[y, h], dev(yy=turn(y, k))) for k in (2, 1, 3)
        ]
        return buf, first, direct

    def gather_tok_end(state):
        buf, first, direct = state
        first.wait_recv()
        passed = [
            send(buf.at[y, 1 - h], buf.at[y, 1 - h], dev(yy=turn(y, k))) for k in (2, 1, 3)
        ]
        for copy in direct + passed:
            copy.wait_recv()

    l_cot.wait()
    l_val.wait()
    bias = mm(var_rows, s.aval[...])
    s.ubias[...] = bias
    row_var = lax.broadcasted_iota(jnp.int32, (128, 256), 0) // PIX
    for n in range(4):
        cols = pl.ds(n * 256, 256)
        u = mm(s.wx[...], s.aval[:, cols])
        for i in range(2):
            s.ub[i, :, cols] = jnp.where(row_var == i, u, 0.0).astype(BF)

    def value_step(i, carry):
        lhs = s.ptl[i].reshape(128, 128)
        for j in range(2):
            out = mm(lhs, s.ub[j]) + s.ubias[j : j + 1, :]
            s.vals[j, i] = out.astype(BF).reshape(NX, 32, WIDTH)
        return carry

    lax.fori_loop(0, 2, value_step, 0)
    for copy in t_near:
        copy.wait_recv()
    near = s.town[...]
    for i in range(7):
        near = near + s.trecv[i].astype(F32)
    s.town[...] = near
    s.tsend[1] = near.astype(BF)
    t_z = [send(s.tsend.at[1], s.trecv.at[6 + k], dev(zz=turn(z, k))) for k in (2, 1, 3)]
    lax.fori_loop(2, 4, value_step, 0)
    for copy in t_z:
        copy.wait_recv()
    total = s.town[...]
    for i in range(7, 10):
        total = total + s.trecv[i].astype(F32)
    probs = s.expo[...] / jnp.concatenate([total, total], axis=0)
    probs = jnp.concatenate([probs, jnp.zeros((96, SPAN), F32)], axis=0)
    s.prl[...] = jnp.transpose(probs).reshape(NZ, NX, 32, 128)

    def sum_var(produce, part, rc, s1, rm, rx, own, s2, rz):
        core, middle, over_x = {}, {}, []
        right, left = dev(xx=turn(x, 1)), dev(xx=turn(x, 3))
        low, high = pl.ds(0, NZ // 2), pl.ds(NZ // 2, NZ // 2)

        def finish(k):
            core[k].wait_recv()
            xk = turn(x, k)
            total = part[:, xk, c].astype(F32) + rc[k].astype(F32)
            if k == 0:
                own[...] = total
                return
            s1[k - 1] = total.astype(BF)
            if k == 2:
                middle[1] = send(s1.at[1, low], rm.at[0], right)
                middle[3] = send(s1.at[1, high], rm.at[1], left)
            if k == 1:
                over_x.append(send(s1.at[0, high], rx.at[0, high], right))
            if k == 3:
                over_x.append(send(s1.at[2, low], rx.at[1, low], left))

        def relay(k):
            middle[k].wait_recv()
            if k == 1:
                s1[0, low] = (s1[0, low].astype(F32) + rm[0].astype(F32)).astype(BF)
                over_x.append(send(s1.at[0, low], rx.at[0, low], right))
            else:
                s1[2, high] = (s1[2, high].astype(F32) + rm[1].astype(F32)).astype(BF)
                over_x.append(send(s1.at[2, high], rx.at[1, high], left))

        previous = None
        for k in (2, 1, 3, 0):
            xk = turn(x, k)
            produce(xk)
            core[k] = send(part.at[:, xk, 1 - c], rc.at[k], sibling)
            if previous is not None:
                finish(previous)
            if previous == 3:
                relay(1)
                relay(3)
            previous = k
        finish(previous)
        for copy in over_x:
            copy.wait_recv()

        def here(zk):
            return own[zk] + rx[0, zk].astype(F32) + rx[1, zk].astype(F32)

        over_z = []
        for k in (2, 1, 3):
            zk = turn(z, k)
            s2[k - 1] = here(zk).astype(BF)
            over_z.append(send(s2.at[k - 1], rz.at[k - 1], dev(zz=zk)))
        mine = here(z)
        for copy in over_z:
            copy.wait_recv()
        return mine + rz[0].astype(F32) + rz[1].astype(F32) + rz[2].astype(F32)

    def pool_produce(xk):
        probs_b = s.prl[:, xk].reshape(128, 128).astype(BF)
        acc = None
        for j in range(2):
            term = mm(probs_b, s.spread[j]) * s.vals[j, :, xk].reshape(128, WIDTH).astype(F32)
            acc = term if acc is None else acc + term
        s.part[:, xk] = acc.astype(BF).reshape(NZ, NC, ROWS, WIDTH)

    cot_state = gather_tok_start(s.cot)
    picked = sum_var(pool_produce, s.part, s.rc1, s.s1, s.rm1, s.rx1, s.own1, s.s2, s.rz1)
    picked_b = picked.astype(BF)
    s.picked[...] = picked_b.astype(F32)

    for copy in l_mix:
        copy.wait()
    x_first = mm(picked_b, s.aout[...]) + s.posv[...].astype(F32)
    s.xa[h] = x_first
    s.xnear[...] = x_first.astype(BF)
    hat, rstd1 = norm_parts(x_first)
    s.xh1[...] = hat
    s.nf1[y, h] = (hat * s.g1[...]).astype(BF)
    state = gather_tok_start(s.nf1)
    gather_tok_end(cot_state)
    x_copy = send(s.xnear, s.xfar, partner)
    gather_tok_end(state)
    for copy in l_qkv:
        copy.wait()
    qkv = mm(s.nf1[...].reshape(128, WIDTH), s.wq[...])
    s.kvb[z, x, c] = qkv[:, 128:384].astype(BF)

    def gather_var_start(buf):
        mine = buf.at[z, x, c]
        right, left = dev(xx=turn(x, 1)), dev(xx=turn(x, 3))
        over_z = [send(mine, mine, dev(zz=turn(z, k))) for k in (1, 2, 3)]
        over_x = {(0, 1): send(mine, mine, right), (0, 3): send(mine, mine, left)}
        over_c = {(0, 0): send(mine, mine, sibling)}
        return buf, over_z, over_x, over_c

    def gather_var_pass(state):
        buf, over_z, over_x, over_c = state
        right, left = dev(xx=turn(x, 1)), dev(xx=turn(x, 3))
        for kz in (1, 3, 2):
            over_z[kz - 1].wait_recv()
            block = buf.at[turn(z, 4 - kz), x, c]
            over_x[kz, 1] = send(block, block, right)
            over_x[kz, 3] = send(block, block, left)
            over_c[kz, 0] = send(block, block, sibling)

    def gather_var_end(state):
        buf, over_z, over_x, over_c = state
        right, left = dev(xx=turn(x, 1)), dev(xx=turn(x, 3))
        for kz in (0, 1, 3, 2):
            for kx in (1, 3):
                over_x[kz, kx].wait_recv()
                block = buf.at[turn(z, 4 - kz), turn(x, 4 - kx), c]
                if kx == 1 and kz in (0, 1):
                    over_x[kz, 2] = send(block, block, right)
                if kx == 3 and kz in (2, 3):
                    over_x[kz, 2] = send(block, block, left)
                over_c[kz, kx] = send(block, block, sibling)

    def gather_var_far(state):
        buf, over_z, over_x, over_c = state
        for kz in (0, 1, 3, 2):
            over_x[kz, 2].wait_recv()
            block = buf.at[turn(z, 4 - kz), turn(x, 2), c]
            over_c[kz, 2] = send(block, block, sibling)

    def gather_var_core(state, kx):
        for kz in range(4):
            state[3][kz, kx].wait_recv()

    kv_state = gather_var_start(s.kvb)
    lane128 = lax.broadcasted_iota(jnp.int32, (128, 128), 1)
    row128 = lax.broadcasted_iota(jnp.int32, (128, 128), 0)

    def by_head(values):
        zero = jnp.zeros_like(values)
        return jnp.concatenate(
            [jnp.where(lane128 < SIZE, values, zero), jnp.where(lane128 >= SIZE, values, zero)],
            axis=0,
        ).astype(BF)

    def own_head(values):
        return jnp.where(row128 < SIZE, values[:, 0:128], values[:, 128:256])

    query = qkv[:, 0:128].astype(BF).astype(F32) * SCALE
    s.qs[...] = by_head(query)
    s.numt[...] = jnp.zeros((128, 256), F32)
    s.tot[...] = jnp.zeros((8, 256), F32)
    gather_var_pass(kv_state)

    def attend(xk):
        def step(i, carry):
            block = s.kvb[pl.ds(i * 2, 2), xk].reshape(512, 256)
            scores = mm_nt(block[:, 0:128], s.qs[...])
            e = jnp.exp(scores)
            e_b = e.astype(BF)
            s.es[xk, pl.ds(i * 2, 2)] = e_b.reshape(2, 256, 256)
            s.tot[...] += jnp.sum(e.reshape(64, 8, 256), axis=0)
            s.numt[...] += mm(jnp.transpose(block[:, 128:256].astype(F32)).astype(BF), e_b)
            return carry

        lax.fori_loop(0, 2, step, 0)

    gather_var_core(kv_state, 0)
    attend(x)
    gather_var_end(kv_state)
    gather_var_core(kv_state, 1)
    attend(turn(x, 3))
    gather_var_far(kv_state)
    gather_var_core(kv_state, 3)
    attend(turn(x, 1))
    gather_var_core(kv_state, 2)
    attend(turn(x, 2))

    inverse = 1.0 / jnp.sum(s.tot[...], axis=0, keepdims=True)
    inv_t = own_head(jnp.broadcast_to(inverse, (128, 256)))
    s.inv[...] = jnp.transpose(inv_t)
    att = jnp.transpose(own_head(s.numt[...]) * inv_t)
    s.att[...] = att

    def sum_tok_start(i, values):
        s.tsrc[i] = values.astype(BF).reshape(NY, NH, ROWS, WIDTH)
        return [
            send(s.tsrc.at[i, turn(y, k)], s.try_.at[i, k - 1], dev(yy=turn(y, k)))
            for k in (2, 1, 3)
        ]

    def sum_tok_pass(i, over_y):
        for copy in over_y:
            copy.wait_recv()

        def here(hh):
            return (
                s.tsrc[i, y, hh].astype(F32)
                + s.try_[i, 0, hh].astype(F32)
                + s.try_[i, 1, hh].astype(F32)
                + s.try_[i, 2, hh].astype(F32)
            )

        s.tsz[i] = here(1 - h).astype(BF)
        copy = send(s.tsz.at[i], s.trz.at[i], partner)
        return copy, here(h)

    def sum_tok_end(i, state):
        copy, mine = state
        copy.wait_recv()
        return mine + s.trz[i].astype(F32)

    def sum_tok_both(i, over_y):
        for copy in over_y:
            copy.wait_recv()
        mine = s.tsrc[i, y].astype(F32)
        for k in range(3):
            mine = mine + s.try_[i, k].astype(F32)
        s.bsz[i] = mine.astype(BF)
        copy = send(s.bsz.at[i], s.brz.at[i], partner)
        copy.wait_recv()
        return (mine + s.brz[i].astype(F32)).reshape(2 * ROWS, WIDTH)

    def gather_y_start(buf):
        return [send(buf.at[y], buf.at[y], dev(yy=turn(y, k))) for k in (2, 1, 3)]

    def both_rows(ref):
        return ref[...].reshape(2 * ROWS, WIDTH)

    l_wo.wait()
    over_y = sum_tok_start(0, mm(att.astype(BF), s.wo[...]))
    for copy in l_mlp:
        copy.wait()
    grad_hidden = mm_nt(s.cot[...].reshape(128, WIDTH), s.wd[...])
    x_copy.wait_recv()
    s.xa[1 - h] = s.xfar[...].astype(F32)
    x_second = both_rows(s.xa) + sum_tok_both(0, over_y)
    s.xb[...] = x_second.reshape(NH, ROWS, WIDTH)
    hat2, rstd2 = norm_parts(x_second)
    s.xh2[...] = hat2.reshape(NH, ROWS, WIDTH)
    s.nf2[y] = (hat2 * s.g2[...]).astype(BF).reshape(NH, ROWS, WIDTH)
    for copy in gather_y_start(s.nf2):
        copy.wait_recv()
    hidden_pre = mm(s.nf2[...].reshape(128, WIDTH), s.wu[...])
    hidden, slope = gelu_both(hidden_pre)
    s.hid[...] = hidden.astype(BF)
    grad_pre = (slope * grad_hidden).astype(BF)
    over_y = sum_tok_start(1, mm_nt(grad_pre, s.wu[...]))
    out_y = sum_tok_start(2, mm(s.hid[...], s.wd[...]))
    grad_normed = sum_tok_both(1, over_y)
    both_cot = s.cot[y].astype(F32).reshape(2 * ROWS, WIDTH)
    grad_second = both_cot + norm_back(grad_normed, both_rows(s.xh2), rstd2, s.g2[...])
    s.gsec[...] = grad_second.reshape(NH, ROWS, WIDTH)
    s.gsa[y] = grad_second.astype(BF).reshape(NH, ROWS, WIDTH)
    over_y = gather_y_start(s.gsa)
    out_state = sum_tok_pass(2, out_y)
    for copy in over_y:
        copy.wait_recv()

    grad_att = mm_nt(s.gsa[...].reshape(128, WIDTH), s.wo[...]).astype(BF)
    grad_over = (grad_att.astype(F32) * s.inv[...]).astype(BF)
    s.gb[...] = by_head(grad_over.astype(F32))
    product = jnp.transpose(grad_over.astype(F32) * s.att[...])
    delta = jnp.concatenate(
        [
            jnp.sum(product[0:SIZE], axis=0, keepdims=True),
            jnp.sum(product[SIZE:128], axis=0, keepdims=True),
        ],
        axis=1,
    )
    s.tot[0:1, :] = delta
    s.numt[...] = jnp.zeros((128, 256), F32)

    def attend_back(xk):
        def step(i, carry):
            block = s.kvb[pl.ds(i * 2, 2), xk].reshape(512, 256)
            e_b = s.es[xk, pl.ds(i * 2, 2)].reshape(512, 256)
            ahead = mm_nt(block[:, 128:256], s.gb[...])
            d_b = (e_b.astype(F32) * (ahead - s.tot[0:1, :])).astype(BF)
            s.numt[...] += mm(jnp.transpose(block[:, 0:128].astype(F32)).astype(BF), d_b)
            grad_key = mm(d_b, s.qs[...]).astype(BF)
            grad_value = mm(e_b, s.gb[...]).astype(BF)
            s.dp[pl.ds(i * 2, 2), xk] = jnp.concatenate([grad_key, grad_value], axis=1).reshape(
                2, NC, 128, 256
            )
            return carry

        lax.fori_loop(0, 2, step, 0)

    own_kv = sum_var(attend_back, s.dp, s.rc2, s.s1b, s.rm2, s.rx2, s.own2, s.s2b, s.rz2)
    grad_query = jnp.transpose(own_head(s.numt[...])) * SCALE
    grad_qkv = jnp.concatenate([grad_query.astype(BF), own_kv.astype(BF)], axis=1)
    over_y = sum_tok_start(3, mm_nt(grad_qkv, s.wq[...]))
    s.out_ref[...] = (s.xb[h] + sum_tok_end(2, out_state)).astype(BF)
    grad_normed = sum_tok_end(3, sum_tok_pass(3, over_y))
    grad_first = s.gsec[h] + norm_back(grad_normed, s.xh1[...], rstd1, s.g1[...])

    grad_picked = mm_nt(grad_first.astype(BF), s.aout[...]).astype(BF)
    inner = mm_nt((grad_picked.astype(F32) * s.picked[...]).astype(BF), s.spread[0] + s.spread[1])
    s.gpb[z, x, c] = jnp.concatenate([grad_picked, inner.astype(BF)], axis=1)
    gp_state = gather_var_start(s.gpb)
    rows_k = lax.broadcasted_iota(jnp.int32, (128, WIDTH), 0)
    keys8 = jnp.concatenate([s.akey[...]] * 8, axis=0)
    s.kext[...] = jnp.where(rows_k < 32, keys8.astype(F32), 0.0).astype(BF)
    gather_var_pass(gp_state)

    def pool_back(xk):
        block = s.gpb[:, xk].reshape(128, GWIDTH)
        grad = block[:, 0:WIDTH].astype(F32)
        probs = s.prl[:, xk].reshape(128, 128)
        probs_b = probs.astype(BF)
        ahead = None
        for j in range(2):
            term = (grad * s.vals[j, :, xk].reshape(128, WIDTH).astype(F32)).astype(BF)
            term = mm_nt(term, s.spread[j])
            ahead = term if ahead is None else ahead + term
            wide = mm(probs_b, s.spread[j])
            s.zs[j, :, xk] = (wide * grad).astype(BF).reshape(NZ, 32, WIDTH)
        scores = probs * (ahead - block[:, WIDTH:GWIDTH].astype(F32)) * SCALE
        s.gps[:, xk] = scores.astype(BF).reshape(NZ, 32, 128)

    gather_var_core(gp_state, 0)
    pool_back(x)
    gather_var_end(gp_state)
    gather_var_core(gp_state, 1)
    pool_back(turn(x, 3))
    gather_var_far(gp_state)
    gather_var_core(gp_state, 3)
    pool_back(turn(x, 1))
    gather_var_core(gp_state, 2)
    pool_back(turn(x, 2))

    key_part = mm(s.px[...].reshape(2 * EXT, SPAN), s.gps[...].reshape(SPAN, 128))
    rows160 = lax.broadcasted_iota(jnp.int32, (2 * EXT, 128), 0) // EXT
    lanes160 = lax.broadcasted_iota(jnp.int32, (2 * EXT, 128), 1) // 16
    key_part = jnp.where(rows160 == lanes160, key_part, 0.0).astype(BF)
    value_part = jnp.concatenate(
        [mm(s.px[j], s.zs[j].reshape(SPAN, WIDTH)).astype(BF) for j in range(2)], axis=0
    )
    for n in range(4):
        cols = pl.ds(n * 256, 256)
        term = mm_nt(value_part, s.aval[cols, :]) + mm(key_part, s.kext[:, cols])
        term = term.astype(BF)
        for i in range(2):
            s.fsrc[n, i] = term[:, i * 128 : (i + 1) * 128]
    last = [
        send(s.fsrc.at[turn(y, k)], s.fry.at[k - 1], dev(yy=turn(y, k))) for k in (2, 1, 3)
    ]
    for copy in last:
        copy.wait_recv()

    def here(hh):
        return (
            s.fsrc[y, hh].astype(F32)
            + s.fry[0, hh].astype(F32)
            + s.fry[1, hh].astype(F32)
            + s.fry[2, hh].astype(F32)
        )

    s.fsz[...] = here(1 - h).astype(BF)
    copy = send(s.fsz, s.frz, partner)
    mine = here(h)
    copy.wait_recv()
    final = mine + s.frz[...].astype(F32)
    s.sum_ref[...] = final
    for copy in started:
        copy.wait_send()


def finish_kernel(out_ref, sum_ref, block_ref, embed_ref, var_ref):
    block_ref[...] = out_ref[...]
    for j in range(2):
        embed_ref[j] = sum_ref[j * EXT : j * EXT + PIX]
        var_ref[j : j + 1, :] = sum_ref[j * EXT + PIX : j * EXT + PIX + 1]


def local(
    patches,
    embed_weight,
    var_embed,
    agg_keys,
    agg_value,
    agg_out,
    pos_embed,
    norm_first,
    norm_second,
    w_qkv,
    w_out,
    w_up,
    w_down,
    cotangent,
):
    anywhere = pl.BlockSpec(memory_space=pl.ANY)
    vmem = pl.BlockSpec(memory_space=pltpu.VMEM)
    results = pl.pallas_call(
        kernel,
        out_shape=(
            jax.ShapeDtypeStruct((ROWS, WIDTH), BF),
            jax.ShapeDtypeStruct((2 * EXT, 128), F32),
        ),
        in_specs=[anywhere] * 14,
        out_specs=(vmem, vmem),
        scratch_shapes=[pltpu.VMEM(shape, dtype) for shape, dtype in SCRATCH.values()]
        + [
            pltpu.SemaphoreType.DMA((LINKS,)),
            pltpu.SemaphoreType.DMA((LINKS,)),
            pltpu.SemaphoreType.DMA((20,)),
        ],
        compiler_params=pltpu.CompilerParams(
            collective_id=0, has_side_effects=True, vmem_limit_bytes=56 * 1024 * 1024
        ),
    )(
        patches,
        embed_weight.reshape(2 * PIX, WIDTH),
        var_embed,
        agg_keys,
        agg_value,
        agg_out,
        pos_embed,
        norm_first.reshape(1, WIDTH),
        norm_second.reshape(1, WIDTH),
        w_qkv,
        w_out,
        w_up,
        w_down,
        cotangent,
    )
    return pl.pallas_call(
        finish_kernel,
        out_shape=(
            jax.ShapeDtypeStruct((ROWS, WIDTH), BF),
            jax.ShapeDtypeStruct((2, PIX, 128), F32),
            jax.ShapeDtypeStruct((2, 128), F32),
        ),
        in_specs=[vmem, vmem],
        out_specs=(vmem, vmem, vmem),
    )(*results)


def solution(mesh):
    in_specs = (
        P("var", None, "tok"),
        P("var", None, None),
        P("var", None),
        P(),
        P(),
        P(),
        P(("tok", "var"), None),
        P(),
        P(),
        P(None, None, "tok"),
        P("tok", None),
        P(None, "tok"),
        P("tok", None),
        P(("tok", "var"), None),
    )
    out_specs = (P(("tok", "var"), None), P("var", None, "tok"), P("var", "tok"))
    return jax.shard_map(local, mesh=mesh, in_specs=in_specs, out_specs=out_specs, check_vma=False)
```

time: 1320 us -> 151 us (0.11)
  waiting for transfers between devices: 915 us -> 0 us
  blocking collectives: 290 us -> 0 us
  Pallas kernels: 0 us -> 150 us
  matrix products: 45 us -> 0 us
  local copies, waits for them, and re-layouts: 34.1 us -> 0 us
  other arithmetic: 19.4 us -> 0 us
  between operations: 14.4 us -> 0.64 us
    reduce_scatter x6 -> x0, waiting for transfers between devices: 577 us -> none  [the longest x1 145 us: local(): lax.psum_scatter(key_terms.reshape(seq, 2, local_width).astype(jnp.bfloat...]
    all_gather x3 -> x0, waiting for transfers between devices: 178 us -> none  [the longest x1 71.2 us: local(): keys_values = lax.all_gather(qkv[:, 1:], 'var', axis=0, tiled=True)]
    unnamed x13 -> x0, waiting for transfers between devices: 161 us -> none
    all_gather x4 -> x0, blocking collectives: 155 us -> none  [the longest x1 39.1 us: local(): lax.all_gather(cotangent, 'tok', axis=0, tiled=True)]
    pallas_call x0 -> x2, Pallas kernels: none -> 150 us  [the longest x1 149 us: local(): pl.pallas_call(kernel, out_shape=(jax.ShapeDtypeStruct((ROWS, WIDTH), BF)...]
    psum x1 -> x0, blocking collectives: 135 us -> none  [local(): pool_total = lax.psum(jnp.sum(expo_pool, axis=0), 'var')]
    dot_general x30 -> x0, matrix products: 44.6 us -> none  [the longest x2 4.44 us: backward_step(): jnp.einsum('hrk,rhe->khe', probs_b, grad_att, preferred_element_type=jnp....]
  transfers between devices with their start and end apart: 11 -> 0, of which waited for: 11 -> 0; matrix products, arithmetic and copies ran while one was open for 1% -> 0% of each run, Pallas kernels for 0% -> 0%
where the time goes in v2:
time: 151 us
  Pallas kernels  150 us (99%)
    pallas_call x1, Pallas kernels, local(): pl.pallas_call(kernel, out_shape=(jax.ShapeDtypeStruct((ROWS, WIDTH), BF)...  149 us

profile of v2, /device:TPU:1, one launch (start us, length us, event | category | flops | bytes accessed | tf_op | source)
XLA Modules:
  0.0 150.9 jit_solution(11274159147633894126)
XLA Ops:
  0.6 148.7 %shard_map.157 = (bf16[16,1024]{1,0:T(8,128)(2,1)}, f32[160,128]{1,0:T(8,128)}) custom-call(bf16[2,64,512]{2,1,0:T(8,128)(2,1)} %refs_0_.1, bf16[128,1024]{1,0:T(8,128)(2,1)} %bitcast.3, f32[2,1024]{1,0:T(2,128)} %refs_2_.1, bf16[16,1024]{1,0:T(8,128)(2,1)} %refs_3_.1, bf16[1024,1024]{1,0:T(8,128)(2,1)} %refs_4_.1, bf16[1024,1024]{1,0:T(8,128)(2,1)} %refs_5_.1, ...), custom_call_target="tpu_custom_call" | custom-call | tf_op jit(solution)/shard_map/pallas_call | solution.py:707
  149.4 1.6 %shard_map.158 = (bf16[16,1024]{1,0:T(8,128)(2,1)}, f32[2,64,128]{2,1,0:T(8,128)}, f32[2,128]{1,0:T(2,128)}) custom-call(bf16[16,1024]{1,0:T(8,128)(2,1)} %get-tuple-element.5.out_ref, f32[160,128]{1,0:T(8,128)} %get-tuple-element.6.sum_ref), custom_call_target="tpu_custom_call" | custom-call | tf_op jit(solution)/shard_map/pallas_call | solution.py:740

commit v3 on v2

--- a/solution.py
+++ b/solution.py
@@ -79,8 +79,7 @@
     part=((NZ, NX, NC, ROWS, WIDTH), BF),
     rc1=((NX, NZ, ROWS, WIDTH), BF),
     s1=((NX - 1, NZ, ROWS, WIDTH), BF),
-    rm1=((2, NZ // 2, ROWS, WIDTH), BF),
-    rx1=((2, NZ, ROWS, WIDTH), BF),
+    rx1=((3, NZ, ROWS, WIDTH), BF),
     own1=((NZ, ROWS, WIDTH), F32),
     s2=((NZ - 1, ROWS, WIDTH), BF),
     rz1=((NZ - 1, ROWS, WIDTH), BF),
@@ -114,15 +113,22 @@
     inv=((128, 128), F32),
     att=((128, 128), F32),
     gb=((256, 128), BF),
-    dp=((NZ, NX, NC, 128, 256), BF),
-    rc2=((NX, NZ, 128, 256), BF),
-    s1b=((NX - 1, NZ, 128, 256), BF),
-    rm2=((2, NZ // 2, 128, 256), BF),
-    rx2=((2, NZ, 128, 256), BF),
-    own2=((NZ, 128, 256), F32),
-    s2b=((NZ - 1, 128, 256), BF),
-    rz2=((NZ - 1, 128, 256), BF),
-    gpre=((128, 512), BF),
+    dpk=((NZ, NX, NC, 128, 128), BF),
+    rck=((NX, NZ, 128, 128), BF),
+    s1k=((NX - 1, NZ, 128, 128), BF),
+    rmk=((2, NZ // 2, 128, 128), BF),
+    rxk=((2, NZ, 128, 128), BF),
+    ownk=((NZ, 128, 128), F32),
+    s2k=((NZ - 1, 128, 128), BF),
+    rzk=((NZ - 1, 128, 128), BF),
+    dpv=((NZ, NX, NC, 128, 128), BF),
+    rcv=((NX, NZ, 128, 128), BF),
+    s1v=((NX - 1, NZ, 128, 128), BF),
+    rmv=((2, NZ // 2, 128, 128), BF),
+    rxv=((2, NZ, 128, 128), BF),
+    ownv=((NZ, 128, 128), F32),
+    s2v=((NZ - 1, 128, 128), BF),
+    rzv=((NZ - 1, 128, 128), BF),
     hid=((128, 512), BF),
     gpb=((NZ, NX, NC, ROWS, GWIDTH), BF),
     zs=((2, NZ, NX, 32, WIDTH), BF),
@@ -197,6 +203,13 @@
         copy.start()
         started.append(copy)
         return copy
+
+    settled = [0, 0]
+
+    def settle():
+        for copy in started[settled[0] : settled[1]]:
+            copy.wait_send()
+        settled[:] = settled[1], len(started)
 
     loads = []
 
@@ -271,6 +284,7 @@
     def gather_tok_end(state):
         buf, first, direct = state
         first.wait_recv()
+        settle()
         passed = [
             send(buf.at[y, 1 - h], buf.at[y, 1 - h], dev(yy=turn(y, k))) for k in (2, 1, 3)
         ]
@@ -314,63 +328,70 @@
     probs = jnp.concatenate([probs, jnp.zeros((96, SPAN), F32)], axis=0)
     s.prl[...] = jnp.transpose(probs).reshape(NZ, NX, 32, 128)
 
-    def sum_var(produce, part, rc, s1, rm, rx, own, s2, rz):
-        core, middle, over_x = {}, {}, []
-        right, left = dev(xx=turn(x, 1)), dev(xx=turn(x, 3))
-        low, high = pl.ds(0, NZ // 2), pl.ds(NZ // 2, NZ // 2)
-
-        def finish(k):
-            core[k].wait_recv()
-            xk = turn(x, k)
-            total = part[:, xk, c].astype(F32) + rc[k].astype(F32)
+    class VarSum:
+        def __init__(self, part, rc, s1, rm, rx, own, s2, rz):
+            self.part, self.rc, self.s1, self.rm = part, rc, s1, rm
+            self.rx, self.own, self.s2, self.rz = rx, own, s2, rz
+            self.core, self.middle, self.over_x, self.over_z = {}, {}, [], []
+            self.right, self.left = dev(xx=turn(x, 1)), dev(xx=turn(x, 3))
+            self.low, self.high = pl.ds(0, NZ // 2), pl.ds(NZ // 2, NZ // 2)
+
+        def put(self, k):
+            self.core[k] = send(self.part.at[:, turn(x, k), 1 - c], self.rc.at[k], sibling)
+
+        def pass_x(self, src, dst, device):
+            self.over_x.append(send(src, dst, device))
+
+        def finish(self, k):
+            self.core[k].wait_recv()
+            s1, rx, low, high = self.s1, self.rx, self.low, self.high
+            total = self.part[:, turn(x, k), c].astype(F32) + self.rc[k].astype(F32)
             if k == 0:
-                own[...] = total
+                self.own[...] = total
                 return
             s1[k - 1] = total.astype(BF)
-            if k == 2:
-                middle[1] = send(s1.at[1, low], rm.at[0], right)
-                middle[3] = send(s1.at[1, high], rm.at[1], left)
-            if k == 1:
-                over_x.append(send(s1.at[0, high], rx.at[0, high], right))
-            if k == 3:
-                over_x.append(send(s1.at[2, low], rx.at[1, low], left))
-
-        def relay(k):
-            middle[k].wait_recv()
-            if k == 1:
-                s1[0, low] = (s1[0, low].astype(F32) + rm[0].astype(F32)).astype(BF)
-                over_x.append(send(s1.at[0, low], rx.at[0, low], right))
+            if self.rm is None:
+                self.pass_x(s1.at[k - 1], rx.at[k - 1], dev(xx=turn(x, k)))
+            elif k == 2:
+                self.middle[1] = send(s1.at[1, low], self.rm.at[0], self.right)
+                self.middle[3] = send(s1.at[1, high], self.rm.at[1], self.left)
+            elif k == 1:
+                self.pass_x(s1.at[0, high], rx.at[0, high], self.right)
             else:
-                s1[2, high] = (s1[2, high].astype(F32) + rm[1].astype(F32)).astype(BF)
-                over_x.append(send(s1.at[2, high], rx.at[1, high], left))
-
-        previous = None
-        for k in (2, 1, 3, 0):
-            xk = turn(x, k)
-            produce(xk)
-            core[k] = send(part.at[:, xk, 1 - c], rc.at[k], sibling)
-            if previous is not None:
-                finish(previous)
-            if previous == 3:
-                relay(1)
-                relay(3)
-            previous = k
-        finish(previous)
-        for copy in over_x:
-            copy.wait_recv()
-
-        def here(zk):
-            return own[zk] + rx[0, zk].astype(F32) + rx[1, zk].astype(F32)
-
-        over_z = []
-        for k in (2, 1, 3):
-            zk = turn(z, k)
-            s2[k - 1] = here(zk).astype(BF)
-            over_z.append(send(s2.at[k - 1], rz.at[k - 1], dev(zz=zk)))
-        mine = here(z)
-        for copy in over_z:
-            copy.wait_recv()
-        return mine + rz[0].astype(F32) + rz[1].astype(F32) + rz[2].astype(F32)
+                self.pass_x(s1.at[2, low], rx.at[1, low], self.left)
+
+        def relay(self):
+            if self.rm is None:
+                return
+            s1, rm, rx, low, high = self.s1, self.rm, self.rx, self.low, self.high
+            self.middle[1].wait_recv()
+            s1[0, low] = (s1[0, low].astype(F32) + rm[0].astype(F32)).astype(BF)
+            self.pass_x(s1.at[0, low], rx.at[0, low], self.right)
+            self.middle[3].wait_recv()
+            s1[2, high] = (s1[2, high].astype(F32) + rm[1].astype(F32)).astype(BF)
+            self.pass_x(s1.at[2, high], rx.at[1, high], self.left)
+
+        def here(self, zk):
+            total = self.own[zk]
+            for i in range(self.rx.shape[0]):
+                total = total + self.rx[i, zk].astype(F32)
+            return total
+
+        def along_z(self):
+            for copy in self.over_x:
+                copy.wait_recv()
+            for k in (2, 1, 3):
+                zk = turn(z, k)
+                self.s2[k - 1] = self.here(zk).astype(BF)
+                self.over_z.append(send(self.s2.at[k - 1], self.rz.at[k - 1], dev(zz=zk)))
+
+        def end(self):
+            mine = self.here(z)
+            settle()
+            for copy in self.over_z:
+                copy.wait_recv()
+            rz = self.rz
+            return mine + rz[0].astype(F32) + rz[1].astype(F32) + rz[2].astype(F32)
 
     def pool_produce(xk):
         probs_b = s.prl[:, xk].reshape(128, 128).astype(BF)
@@ -381,7 +402,16 @@
         s.part[:, xk] = acc.astype(BF).reshape(NZ, NC, ROWS, WIDTH)
 
     cot_state = gather_tok_start(s.cot)
-    picked = sum_var(pool_produce, s.part, s.rc1, s.s1, s.rm1, s.rx1, s.own1, s.s2, s.rz1)
+    pool_sum = VarSum(s.part, s.rc1, s.s1, None, s.rx1, s.own1, s.s2, s.rz1)
+    for k, before in ((2, None), (1, 2), (3, 1), (0, 3)):
+        pool_produce(turn(x, k))
+        pool_sum.put(k)
+        if before is not None:
+            pool_sum.finish(before)
+    pool_sum.finish(0)
+    settle()
+    pool_sum.along_z()
+    picked = pool_sum.end()
     picked_b = picked.astype(BF)
     s.picked[...] = picked_b.astype(F32)
 
@@ -402,39 +432,44 @@
     qkv = mm(s.nf1[...].reshape(128, WIDTH), s.wq[...])
     s.kvb[z, x, c] = qkv[:, 128:384].astype(BF)
 
-    def gather_var_start(buf):
+    def gather_var_start(buf, direct):
         mine = buf.at[z, x, c]
         right, left = dev(xx=turn(x, 1)), dev(xx=turn(x, 3))
         over_z = [send(mine, mine, dev(zz=turn(z, k))) for k in (1, 2, 3)]
         over_x = {(0, 1): send(mine, mine, right), (0, 3): send(mine, mine, left)}
+        if direct:
+            over_x[0, 2] = send(mine, mine, dev(xx=turn(x, 2)))
         over_c = {(0, 0): send(mine, mine, sibling)}
-        return buf, over_z, over_x, over_c
+        settle()
+        return buf, over_z, over_x, over_c, direct
 
     def gather_var_pass(state):
-        buf, over_z, over_x, over_c = state
+        buf, over_z, over_x, over_c, direct = state
         right, left = dev(xx=turn(x, 1)), dev(xx=turn(x, 3))
         for kz in (1, 3, 2):
             over_z[kz - 1].wait_recv()
             block = buf.at[turn(z, 4 - kz), x, c]
             over_x[kz, 1] = send(block, block, right)
             over_x[kz, 3] = send(block, block, left)
+            if direct:
+                over_x[kz, 2] = send(block, block, dev(xx=turn(x, 2)))
             over_c[kz, 0] = send(block, block, sibling)
 
     def gather_var_end(state):
-        buf, over_z, over_x, over_c = state
+        buf, over_z, over_x, over_c, direct = state
         right, left = dev(xx=turn(x, 1)), dev(xx=turn(x, 3))
         for kz in (0, 1, 3, 2):
             for kx in (1, 3):
                 over_x[kz, kx].wait_recv()
                 block = buf.at[turn(z, 4 - kz), turn(x, 4 - kx), c]
-                if kx == 1 and kz in (0, 1):
+                if kx == 1 and kz in (0, 1) and not direct:
                     over_x[kz, 2] = send(block, block, right)
-                if kx == 3 and kz in (2, 3):
+                if kx == 3 and kz in (2, 3) and not direct:
                     over_x[kz, 2] = send(block, block, left)
                 over_c[kz, kx] = send(block, block, sibling)
 
     def gather_var_far(state):
-        buf, over_z, over_x, over_c = state
+        buf, over_z, over_x, over_c, direct = state
         for kz in (0, 1, 3, 2):
             over_x[kz, 2].wait_recv()
             block = buf.at[turn(z, 4 - kz), turn(x, 2), c]
@@ -444,7 +479,7 @@
         for kz in range(4):
             state[3][kz, kx].wait_recv()
 
-    kv_state = gather_var_start(s.kvb)
+    kv_state = gather_var_start(s.kvb, False)
     lane128 = lax.broadcasted_iota(jnp.int32, (128, 128), 1)
     row128 = lax.broadcasted_iota(jnp.int32, (128, 128), 0)
 
@@ -465,7 +500,7 @@
     gather_var_pass(kv_state)
 
     def attend(xk):
-        def step(i, carry):
+        def step(i):
             block = s.kvb[pl.ds(i * 2, 2), xk].reshape(512, 256)
             scores = mm_nt(block[:, 0:128], s.qs[...])
             e = jnp.exp(scores)
@@ -473,13 +508,13 @@
             s.es[xk, pl.ds(i * 2, 2)] = e_b.reshape(2, 256, 256)
             s.tot[...] += jnp.sum(e.reshape(64, 8, 256), axis=0)
             s.numt[...] += mm(jnp.transpose(block[:, 128:256].astype(F32)).astype(BF), e_b)
-            return carry
-
-        lax.fori_loop(0, 2, step, 0)
-
+
+        for i in range(2):
+            step(i)
+
+    gather_var_end(kv_state)
     gather_var_core(kv_state, 0)
     attend(x)
-    gather_var_end(kv_state)
     gather_var_core(kv_state, 1)
     attend(turn(x, 3))
     gather_var_far(kv_state)
@@ -522,7 +557,7 @@
         copy.wait_recv()
         return mine + s.trz[i].astype(F32)
 
-    def sum_tok_both(i, over_y):
+    def sum_tok_both(i, over_y, beside=None):
         for copy in over_y:
             copy.wait_recv()
         mine = s.tsrc[i, y].astype(F32)
@@ -530,6 +565,9 @@
             mine = mine + s.try_[i, k].astype(F32)
         s.bsz[i] = mine.astype(BF)
         copy = send(s.bsz.at[i], s.brz.at[i], partner)
+        if beside is not None:
+            beside()
+        settle()
         copy.wait_recv()
         return (mine + s.brz[i].astype(F32)).reshape(2 * ROWS, WIDTH)
 
@@ -551,20 +589,27 @@
     hat2, rstd2 = norm_parts(x_second)
     s.xh2[...] = hat2.reshape(NH, ROWS, WIDTH)
     s.nf2[y] = (hat2 * s.g2[...]).astype(BF).reshape(NH, ROWS, WIDTH)
-    for copy in gather_y_start(s.nf2):
+    over_y = gather_y_start(s.nf2)
+    settle()
+    for copy in over_y:
         copy.wait_recv()
     hidden_pre = mm(s.nf2[...].reshape(128, WIDTH), s.wu[...])
     hidden, slope = gelu_both(hidden_pre)
     s.hid[...] = hidden.astype(BF)
     grad_pre = (slope * grad_hidden).astype(BF)
     over_y = sum_tok_start(1, mm_nt(grad_pre, s.wu[...]))
-    out_y = sum_tok_start(2, mm(s.hid[...], s.wd[...]))
-    grad_normed = sum_tok_both(1, over_y)
+    out_y = []
+
+    def out_start():
+        out_y.extend(sum_tok_start(2, mm(s.hid[...], s.wd[...])))
+
+    grad_normed = sum_tok_both(1, over_y, out_start)
     both_cot = s.cot[y].astype(F32).reshape(2 * ROWS, WIDTH)
     grad_second = both_cot + norm_back(grad_normed, both_rows(s.xh2), rstd2, s.g2[...])
     s.gsec[...] = grad_second.reshape(NH, ROWS, WIDTH)
     s.gsa[y] = grad_second.astype(BF).reshape(NH, ROWS, WIDTH)
     over_y = gather_y_start(s.gsa)
+    settle()
     out_state = sum_tok_pass(2, out_y)
     for copy in over_y:
         copy.wait_recv()
@@ -583,25 +628,53 @@
     s.tot[0:1, :] = delta
     s.numt[...] = jnp.zeros((128, 256), F32)
 
-    def attend_back(xk):
-        def step(i, carry):
-            block = s.kvb[pl.ds(i * 2, 2), xk].reshape(512, 256)
-            e_b = s.es[xk, pl.ds(i * 2, 2)].reshape(512, 256)
+    def value_back(xk):
+        for i in range(2):
+            pair = pl.ds(i * 2, 2)
+            e_b = s.es[xk, pair].reshape(512, 256)
+            s.dpv[pair, xk] = mm(e_b, s.gb[...]).astype(BF).reshape(2, NC, 128, 128)
+
+    def key_back(xk):
+        for i in range(2):
+            pair = pl.ds(i * 2, 2)
+            block = s.kvb[pair, xk].reshape(512, 256)
+            e_b = s.es[xk, pair].reshape(512, 256)
             ahead = mm_nt(block[:, 128:256], s.gb[...])
             d_b = (e_b.astype(F32) * (ahead - s.tot[0:1, :])).astype(BF)
+            s.dpk[pair, xk] = mm(d_b, s.qs[...]).astype(BF).reshape(2, NC, 128, 128)
             s.numt[...] += mm(jnp.transpose(block[:, 0:128].astype(F32)).astype(BF), d_b)
-            grad_key = mm(d_b, s.qs[...]).astype(BF)
-            grad_value = mm(e_b, s.gb[...]).astype(BF)
-            s.dp[pl.ds(i * 2, 2), xk] = jnp.concatenate([grad_key, grad_value], axis=1).reshape(
-                2, NC, 128, 256
-            )
-            return carry
-
-        lax.fori_loop(0, 2, step, 0)
-
-    own_kv = sum_var(attend_back, s.dp, s.rc2, s.s1b, s.rm2, s.rx2, s.own2, s.s2b, s.rz2)
+
+    v_sum = VarSum(s.dpv, s.rcv, s.s1v, s.rmv, s.rxv, s.ownv, s.s2v, s.rzv)
+    k_sum = VarSum(s.dpk, s.rck, s.s1k, s.rmk, s.rxk, s.ownk, s.s2k, s.rzk)
+    for k, before in ((2, None), (1, 2), (3, 1), (0, 3)):
+        value_back(turn(x, k))
+        v_sum.put(k)
+        if before is not None:
+            v_sum.finish(before)
+    key_back(turn(x, 2))
+    k_sum.put(2)
+    v_sum.finish(0)
+    v_sum.relay()
+    key_back(turn(x, 1))
+    k_sum.put(1)
+    k_sum.finish(2)
+    key_back(turn(x, 3))
+    k_sum.put(3)
+    k_sum.finish(1)
+    key_back(x)
+    k_sum.put(0)
+    k_sum.finish(3)
+    k_sum.relay()
+    k_sum.finish(0)
+    settle()
+    v_sum.along_z()
+    k_sum.along_z()
+    own_v = v_sum.end()
+    own_k = k_sum.end()
     grad_query = jnp.transpose(own_head(s.numt[...])) * SCALE
-    grad_qkv = jnp.concatenate([grad_query.astype(BF), own_kv.astype(BF)], axis=1)
+    grad_qkv = jnp.concatenate(
+        [grad_query.astype(BF), own_k.astype(BF), own_v.astype(BF)], axis=1
+    )
     over_y = sum_tok_start(3, mm_nt(grad_qkv, s.wq[...]))
     s.out_ref[...] = (s.xb[h] + sum_tok_end(2, out_state)).astype(BF)
     grad_normed = sum_tok_end(3, sum_tok_pass(3, over_y))
@@ -610,7 +683,7 @@
     grad_picked = mm_nt(grad_first.astype(BF), s.aout[...]).astype(BF)
     inner = mm_nt((grad_picked.astype(F32) * s.picked[...]).astype(BF), s.spread[0] + s.spread[1])
     s.gpb[z, x, c] = jnp.concatenate([grad_picked, inner.astype(BF)], axis=1)
-    gp_state = gather_var_start(s.gpb)
+    gp_state = gather_var_start(s.gpb, True)
     rows_k = lax.broadcasted_iota(jnp.int32, (128, WIDTH), 0)
     keys8 = jnp.concatenate([s.akey[...]] * 8, axis=0)
     s.kext[...] = jnp.where(rows_k < 32, keys8.astype(F32), 0.0).astype(BF)
@@ -631,9 +704,9 @@
         scores = probs * (ahead - block[:, WIDTH:GWIDTH].astype(F32)) * SCALE
         s.gps[:, xk] = scores.astype(BF).reshape(NZ, 32, 128)
 
+    gather_var_end(gp_state)
     gather_var_core(gp_state, 0)
     pool_back(x)
-    gather_var_end(gp_state)
     gather_var_core(gp_state, 1)
     pool_back(turn(x, 3))
     gather_var_far(gp_state)
@@ -658,6 +731,7 @@
     last = [
         send(s.fsrc.at[turn(y, k)], s.fry.at[k - 1], dev(yy=turn(y, k))) for k in (2, 1, 3)
     ]
+    settle()
     for copy in last:
         copy.wait_recv()
 
@@ -672,10 +746,11 @@
     s.fsz[...] = here(1 - h).astype(BF)
     copy = send(s.fsz, s.frz, partner)
     mine = here(h)
+    settle()
     copy.wait_recv()
     final = mine + s.frz[...].astype(F32)
     s.sum_ref[...] = final
-    for copy in started:
+    for copy in started[settled[0] :]:
         copy.wait_send()
 
 

time: 151 us -> 149 us (0.987)
  Pallas kernels: 150 us -> 148 us
    pallas_call x1, Pallas kernels: 149 us -> 147 us  [local(): pl.pallas_call(kernel, out_shape=(jax.ShapeDtypeStruct((ROWS, WIDTH), BF)...]
where the time goes in v3:
time: 149 us
  Pallas kernels  148 us (99%)
    pallas_call x1, Pallas kernels, local(): pl.pallas_call(kernel, out_shape=(jax.ShapeDtypeStruct((ROWS, WIDTH), BF)...  147 us

profile of v3, /device:TPU:1, one launch (start us, length us, event | category | flops | bytes accessed | tf_op | source)
XLA Modules:
  0.0 149.0 jit_solution(14231332376173290766)
XLA Ops:
  0.6 146.8 %shard_map.157 = (bf16[16,1024]{1,0:T(8,128)(2,1)}, f32[160,128]{1,0:T(8,128)}) custom-call(bf16[2,64,512]{2,1,0:T(8,128)(2,1)} %refs_0_.1, bf16[128,1024]{1,0:T(8,128)(2,1)} %bitcast.3, f32[2,1024]{1,0:T(2,128)} %refs_2_.1, bf16[16,1024]{1,0:T(8,128)(2,1)} %refs_3_.1, bf16[1024,1024]{1,0:T(8,128)(2,1)} %refs_4_.1, bf16[1024,1024]{1,0:T(8,128)(2,1)} %refs_5_.1, ...), custom_call_target="tpu_custom_call" | custom-call | tf_op jit(solution)/shard_map/pallas_call | solution.py:782
  147.5 1.6 %shard_map.158 = (bf16[16,1024]{1,0:T(8,128)(2,1)}, f32[2,64,128]{2,1,0:T(8,128)}, f32[2,128]{1,0:T(2,128)}) custom-call(bf16[16,1024]{1,0:T(8,128)(2,1)} %get-tuple-element.5.out_ref, f32[160,128]{1,0:T(8,128)} %get-tuple-element.6.sum_ref), custom_call_target="tpu_custom_call" | custom-call | tf_op jit(solution)/shard_map/pallas_call | solution.py:815

commit v4 on v3

--- a/solution.py
+++ b/solution.py
@@ -479,7 +479,7 @@
         for kz in range(4):
             state[3][kz, kx].wait_recv()
 
-    kv_state = gather_var_start(s.kvb, False)
+    kv_state = gather_var_start(s.kvb, True)
     lane128 = lax.broadcasted_iota(jnp.int32, (128, 128), 1)
     row128 = lax.broadcasted_iota(jnp.int32, (128, 128), 0)
 

time: 149 us -> 148 us (level)
  no operation moved by 1% of the time
where the time goes in v4:
time: 148 us
  Pallas kernels  147 us (99%)
    pallas_call x1, Pallas kernels, local(): pl.pallas_call(kernel, out_shape=(jax.ShapeDtypeStruct((ROWS, WIDTH), BF)...  146 us

profile of v4, /device:TPU:1, one launch (start us, length us, event | category | flops | bytes accessed | tf_op | source)
XLA Modules:
  0.0 147.8 jit_solution(11982558501933255898)
XLA Ops:
  0.6 145.6 %shard_map.157 = (bf16[16,1024]{1,0:T(8,128)(2,1)}, f32[160,128]{1,0:T(8,128)}) custom-call(bf16[2,64,512]{2,1,0:T(8,128)(2,1)} %refs_0_.1, bf16[128,1024]{1,0:T(8,128)(2,1)} %bitcast.3, f32[2,1024]{1,0:T(2,128)} %refs_2_.1, bf16[16,1024]{1,0:T(8,128)(2,1)} %refs_3_.1, bf16[1024,1024]{1,0:T(8,128)(2,1)} %refs_4_.1, bf16[1024,1024]{1,0:T(8,128)(2,1)} %refs_5_.1, ...), custom_call_target="tpu_custom_call" | custom-call | tf_op jit(solution)/shard_map/pallas_call | solution.py:782
  146.3 1.6 %shard_map.158 = (bf16[16,1024]{1,0:T(8,128)(2,1)}, f32[2,64,128]{2,1,0:T(8,128)}, f32[2,128]{1,0:T(2,128)}) custom-call(bf16[16,1024]{1,0:T(8,128)(2,1)} %get-tuple-element.5.out_ref, f32[160,128]{1,0:T(8,128)} %get-tuple-element.6.sum_ref), custom_call_target="tpu_custom_call" | custom-call | tf_op jit(solution)/shard_map/pallas_call | solution.py:815
